TPU v7x, 32 devices: a whole 2x2x4 slice. The times are simulated.
32 devices in a mesh: item: 8 (over z, x), seq: 4 (over y, core).
Axes of the slice: x: 2, y: 2, z: 4, core: 2. Of those that a mesh axis runs over, the one named last changes fastest.
Arguments:
- inputs: bfloat16 [8, 3072, 768], P('item', 'seq'), may hold values from -6 to 6
- d_output: bfloat16 [8, 3072, 768], P('item', 'seq'), may hold values from -6 to 6
- glob_count: int32 [8], P('item'), may hold values from 2 to 4
- glob_pos: int32 [8, 4], P('item'), may hold values from 0 to 47, as said below
- rand_blocks: int32 [8, 12, 48, 3], P('item', 'seq'), may hold values from 0 to 47
- w_qkv: float32 [768, 2304], P('item'), may hold values from -0.21875 to 0.21875
- w_out: float32 [768, 768], P('item'), may hold values from -0.875 to 0.875
- w_up: float32 [768, 3072], P('item'), may hold values from -0.21875 to 0.21875
- w_down: float32 [3072, 768], P('item'), may hold values from -0.109375 to 0.109375
- small_params: float32 [12, 768], replicated
- first_qkv: float32 [768, 2304], P('item'), may hold values from -0.00024414062 to 0.00024414062
- second_qkv: float32 [768, 2304], P('item'), may hold values from 1.4110135e-10 to 5.644054e-10
- first_out: float32 [768, 768], P('item'), may hold values from -0.00024414062 to 0.00024414062
- second_out: float32 [768, 768], P('item'), may hold values from 1.4110135e-10 to 5.644054e-10
- first_up: float32 [768, 3072], P('item'), may hold values from -0.00024414062 to 0.00024414062
- second_up: float32 [768, 3072], P('item'), may hold values from 1.4110135e-10 to 5.644054e-10
- first_down: float32 [3072, 768], P('item'), may hold values from -0.00024414062 to 0.00024414062
- second_down: float32 [3072, 768], P('item'), may hold values from 1.4110135e-10 to 5.644054e-10
- first_small: float32 [12, 768], replicated, may hold values from -0.0007324219 to 0.0007324219
- second_small: float32 [12, 768], replicated, may hold values from 1.2699122e-09 to 5.0796487e-09
Outputs:
- outputs: bfloat16 [8, 3072, 768], P('item', 'seq')
- d_inputs: float32 [8, 3072, 768], P('item', 'seq')
- grad_norm: float32 [], replicated
- new_w_qkv: float32 [768, 2304], P('item')
- new_first_qkv: float32 [768, 2304], P('item')
- new_second_qkv: float32 [768, 2304], P('item')
- new_w_out: float32 [768, 768], P('item')
- new_first_out: float32 [768, 768], P('item')
- new_second_out: float32 [768, 768], P('item')
- new_w_up: float32 [768, 3072], P('item')
- new_first_up: float32 [768, 3072], P('item')
- new_second_up: float32 [768, 3072], P('item')
- new_w_down: float32 [3072, 768], P('item')
- new_first_down: float32 [3072, 768], P('item')
- new_second_down: float32 [3072, 768], P('item')
- new_small: float32 [12, 768], replicated
- new_first_small: float32 [12, 768], replicated
- new_second_small: float32 [12, 768], replicated
Inputs may be any that keep to these rules, and one draw needn't show every extreme that they name: `glob_pos`: each row holds distinct blocks; its first two entries are block 0 and block 47; only the first glob_count entries of a row are global.
All inputs are finite; a program needn't handle non-finite values.
Results may differ from a plain program's by a relative error of at most 0.012.
The roundings to bfloat16 on the way count: a program that leaves them out, or rounds other values in their place, can miss the bound.
Values may be sent and summed in bfloat16 or wider, within the bound.
A program may use at most 192 MiB of HBM per device.

v0:
```python
import jax
import jax.numpy as jnp
from jax import lax
from jax.sharding import PartitionSpec as P

HEAD_DIM = 64
BLOCK = 64
ADAM_STEP = 10


norm_epsilon = 1e-06
beta_first = 0.9
beta_second = 0.999
adam_epsilon = 1e-08
learn_rate = 0.1
small_rate = 0.5
weight_decay = 0.01
clip_level = 1.0
masked_value = -1e30


def shortened(array):
    return jax.tree.map(lambda a: a.astype(jnp.bfloat16) if a.dtype == jnp.float32 else a, array)


def layer_norm(values, gain, bias):
    average = jnp.mean(values, -1, keepdims=True)
    centered = values - average
    spread = jnp.mean(centered * centered, -1, keepdims=True)
    return centered * lax.rsqrt(spread + norm_epsilon) * gain + bias


def exact_gelu(values):
    return jax.nn.gelu(values, approximate=False)


def block_allowed(count, positions, random_table):
    nblocks = random_table.shape[1]
    block_ids = jnp.arange(nblocks, dtype=jnp.int32)
    active = jnp.arange(positions.shape[0], dtype=jnp.int32) < count
    is_global = jnp.any((positions[:, None] == block_ids[None, :]) & active[:, None], axis=0)
    window = jnp.abs(block_ids[:, None] - block_ids[None, :]) <= 1
    chosen = jnp.any(random_table[:, :, :, None] == block_ids[None, None, None, :], axis=2)
    return window[None] | chosen | is_global[None, :, None] | is_global[None, None, :]


def masked_scores(q_block, k_head, allowed_rows):
    q_rows = q_block.shape[0]
    seq_len = k_head.shape[0]
    scale = q_block.shape[1] ** (-0.5)
    scores = jnp.einsum("qd,kd->qk", q_block, k_head, preferred_element_type=jnp.float32) * scale
    shaped = scores.reshape(q_rows // BLOCK, BLOCK, seq_len // BLOCK, BLOCK)
    shaped = jnp.where(allowed_rows[:, None, :, None], shaped, masked_value)
    return shaped.reshape(q_rows, seq_len)


def head_forward(q_head, k_head, v_head, allowed):
    seq_len = q_head.shape[0]
    q_rows = min(512, seq_len)
    offsets = jnp.arange(seq_len // q_rows, dtype=jnp.int32) * q_rows

    def rows_forward(offset):
        q_block = lax.dynamic_slice_in_dim(q_head, offset, q_rows, 0)
        allowed_rows = lax.dynamic_slice_in_dim(allowed, offset // BLOCK, q_rows // BLOCK, 0)
        scores = masked_scores(q_block, k_head, allowed_rows)
        row_peak = jnp.max(scores, -1, keepdims=True)
        shifted = jnp.exp(scores - row_peak)
        row_total = jnp.sum(shifted, -1, keepdims=True)
        attn_prob = (shifted / row_total).astype(jnp.bfloat16)
        mixed = jnp.dot(attn_prob, v_head, preferred_element_type=jnp.float32)
        return (mixed.astype(jnp.bfloat16), (row_peak + jnp.log(row_total))[:, 0])

    mixed, log_total = lax.map(rows_forward, offsets)
    return (mixed.reshape(seq_len, -1), log_total.reshape(seq_len))


def head_backward(q_head, k_head, v_head, grad_head, log_total, allowed):
    seq_len, head_dim = q_head.shape
    q_rows = min(512, seq_len)
    scale = head_dim ** (-0.5)
    offsets = jnp.arange(seq_len // q_rows, dtype=jnp.int32) * q_rows

    def rows_backward(carried, offset):
        grad_k, grad_v = carried
        q_block = lax.dynamic_slice_in_dim(q_head, offset, q_rows, 0)
        grad_block = lax.dynamic_slice_in_dim(grad_head, offset, q_rows, 0)
        log_block = lax.dynamic_slice_in_dim(log_total, offset, q_rows, 0)
        allowed_rows = lax.dynamic_slice_in_dim(allowed, offset // BLOCK, q_rows // BLOCK, 0)
        scores = masked_scores(q_block, k_head, allowed_rows)
        attn_prob = jnp.exp(scores - log_block[:, None])
        grad_prob = jnp.einsum("qd,kd->qk", grad_block, v_head, preferred_element_type=jnp.float32)
        inner = jnp.sum(grad_prob * attn_prob, -1, keepdims=True)
        grad_score = (attn_prob * (grad_prob - inner)).astype(jnp.bfloat16)
        grad_q = jnp.dot(grad_score, k_head, preferred_element_type=jnp.float32) * scale
        grad_k = (
            grad_k
            + jnp.einsum("qk,qd->kd", grad_score, q_block, preferred_element_type=jnp.float32)
            * scale
        )
        grad_v = grad_v + jnp.einsum(
            "qk,qd->kd",
            attn_prob.astype(jnp.bfloat16),
            grad_block,
            preferred_element_type=jnp.float32,
        )
        return ((grad_k, grad_v), grad_q)

    zero_rows = jnp.zeros((seq_len, head_dim), jnp.float32)
    (grad_k, grad_v), grad_q = lax.scan(rows_backward, (zero_rows, zero_rows), offsets)
    return (grad_q.reshape(seq_len, head_dim), grad_k, grad_v)


def attend_item(packed):
    headwise, count, positions, table = packed
    allowed = block_allowed(count, positions, table)
    mixed_heads = []
    log_heads = []
    for head_num in range(table.shape[0]):
        columns = slice(head_num * HEAD_DIM, (head_num + 1) * HEAD_DIM)
        mixed, log_total = head_forward(
            headwise[:, 0, 0, columns],
            headwise[:, 1, 0, columns],
            headwise[:, 2, 0, columns],
            allowed[head_num],
        )
        mixed_heads.append(mixed)
        log_heads.append(log_total)
    return (jnp.concatenate(mixed_heads, -1), jnp.stack(log_heads))


def attend_back(packed):
    headwise, grad_heads, log_heads, count, positions, table = packed
    allowed = block_allowed(count, positions, table)
    grad_qs = []
    grad_ks = []
    grad_vs = []
    for head_num in range(table.shape[0]):
        columns = slice(head_num * HEAD_DIM, (head_num + 1) * HEAD_DIM)
        grad_q, grad_k, grad_v = head_backward(
            headwise[:, 0, 0, columns],
            headwise[:, 1, 0, columns],
            headwise[:, 2, 0, columns],
            grad_heads[:, 0, columns],
            log_heads[head_num],
            allowed[head_num],
        )
        grad_qs.append(grad_q)
        grad_ks.append(grad_k)
        grad_vs.append(grad_v)
    stacked = jnp.stack(
        [jnp.concatenate(grad_qs, -1), jnp.concatenate(grad_ks, -1), jnp.concatenate(grad_vs, -1)],
        1,
    )
    return stacked[:, :, None, :].astype(jnp.bfloat16)


def adam_update(weight, first, second, grad, decay, rate):
    first_new = beta_first * first + (1.0 - beta_first) * grad
    second_new = beta_second * second + (1.0 - beta_second) * grad * grad
    first_hat = first_new / (1.0 - beta_first**ADAM_STEP)
    second_hat = second_new / (1.0 - beta_second**ADAM_STEP)
    weight_new = weight - rate * (
        first_hat / (jnp.sqrt(second_hat) + adam_epsilon) + decay * weight
    )
    return (weight_new, first_new, second_new)


def on_device(
    inputs,
    d_output,
    glob_count,
    glob_pos,
    rand_blocks,
    w_qkv,
    w_out,
    w_up,
    w_down,
    small_params,
    first_qkv,
    second_qkv,
    first_out,
    second_out,
    first_up,
    second_up,
    first_down,
    second_down,
    first_small,
    second_small,
):
    items_n, tok_rows, width = inputs.shape
    groups = lax.axis_size("seq")
    heads_here = rand_blocks.shape[1]
    head_width = heads_here * HEAD_DIM
    row_count = items_n * tok_rows
    bf16 = jnp.bfloat16
    f32 = jnp.float32
    full_qkv, full_out, full_up, full_down = (
        lax.all_gather(w_qkv.astype(bf16), "item", axis=0, tiled=True),
        lax.all_gather(w_out.astype(bf16), "item", axis=0, tiled=True),
        lax.all_gather(w_up.astype(bf16), "item", axis=0, tiled=True),
        lax.all_gather(w_down.astype(bf16), "item", axis=0, tiled=True),
    )
    tokens_b = inputs.reshape(row_count, width)
    tokens_f = tokens_b.astype(f32)
    zero_bias = jnp.zeros((width,), f32)
    qkv_bias = jnp.concatenate([small_params[2], zero_bias, small_params[3]])
    qkv = (jnp.dot(tokens_b, full_qkv, preferred_element_type=f32) + qkv_bias).astype(bf16)
    headwise = lax.all_to_all(
        qkv.reshape(items_n, tok_rows, 3, groups, head_width),
        "seq",
        split_axis=3,
        concat_axis=1,
        tiled=True,
    )
    mixed_heads, log_heads = lax.map(attend_item, (headwise, glob_count, glob_pos, rand_blocks))
    mixed = lax.all_to_all(
        shortened(mixed_heads.reshape(items_n, tok_rows * groups, 1, head_width)),
        "seq",
        split_axis=1,
        concat_axis=2,
        tiled=True,
    ).reshape(row_count, width)
    attn_out = jnp.dot(mixed, full_out, preferred_element_type=f32) + small_params[4]
    hidden, norm_one_back = jax.vjp(
        layer_norm, tokens_f + attn_out, small_params[0], small_params[1]
    )
    hidden_b = hidden.astype(bf16)
    up_pre = jnp.dot(hidden_b, full_up, preferred_element_type=f32) + small_params[8:12].reshape(-1)
    active, gelu_back = jax.vjp(exact_gelu, up_pre)
    active_b = active.astype(bf16)
    ffn_out = jnp.dot(active_b, full_down, preferred_element_type=f32) + small_params[7]
    outputs, norm_two_back = jax.vjp(layer_norm, hidden + ffn_out, small_params[5], small_params[6])
    grad_second, grad_gain_two, grad_bias_two = norm_two_back(
        d_output.reshape(row_count, width).astype(f32)
    )
    grad_ffn = grad_second.astype(bf16)
    grad_w_down = jnp.einsum("rf,rd->fd", active_b, grad_ffn, preferred_element_type=f32)
    grad_active = jnp.einsum("rd,fd->rf", grad_ffn, full_down, preferred_element_type=f32)
    (grad_up_pre,) = gelu_back(grad_active)
    grad_up_b = grad_up_pre.astype(bf16)
    grad_w_up = jnp.einsum("rd,rf->df", hidden_b, grad_up_b, preferred_element_type=f32)
    grad_hidden = grad_second + jnp.einsum(
        "rf,df->rd", grad_up_b, full_up, preferred_element_type=f32
    )
    grad_first, grad_gain_one, grad_bias_one = norm_one_back(grad_hidden)
    grad_attn = grad_first.astype(bf16)
    grad_w_out = jnp.einsum("rm,rd->md", mixed, grad_attn, preferred_element_type=f32)
    grad_mixed = jnp.einsum("rd,md->rm", grad_attn, full_out, preferred_element_type=f32).astype(
        bf16
    )
    grad_heads = lax.all_to_all(
        grad_mixed.reshape(items_n, tok_rows, groups, head_width),
        "seq",
        split_axis=2,
        concat_axis=1,
        tiled=True,
    )
    grad_qkv_heads = lax.map(
        attend_back, (headwise, grad_heads, log_heads, glob_count, glob_pos, rand_blocks)
    )
    grad_qkv = jax.tree.map(
        lambda part, own: part.astype(own.dtype),
        lax.all_to_all(shortened(grad_qkv_heads), "seq", split_axis=1, concat_axis=3, tiled=True),
        grad_qkv_heads,
    ).reshape(row_count, 3 * width)
    grad_w_qkv = jnp.einsum("rd,re->de", tokens_b, grad_qkv, preferred_element_type=f32)
    grad_inputs = grad_first + jnp.einsum(
        "re,de->rd", grad_qkv, full_qkv, preferred_element_type=f32
    )
    grad_qkv_sum = jnp.sum(grad_qkv.astype(f32), 0)
    small_rows = jnp.stack(
        [
            grad_gain_one,
            grad_bias_one,
            grad_qkv_sum[:width],
            grad_qkv_sum[2 * width :],
            jnp.sum(grad_attn.astype(f32), 0),
            grad_gain_two,
            grad_bias_two,
            jnp.sum(grad_ffn.astype(f32), 0),
        ]
    )
    small_part = jnp.concatenate(
        [small_rows, jnp.sum(grad_up_b.astype(f32), 0).reshape(4, width)], 0
    )
    small_total = lax.psum(small_part, ("item", "seq"))
    shard_qkv, shard_out, shard_up, shard_down = (
        lax.psum_scatter(grad_w_qkv, "item", scatter_dimension=0, tiled=True),
        lax.psum_scatter(grad_w_out, "item", scatter_dimension=0, tiled=True),
        lax.psum_scatter(grad_w_up, "item", scatter_dimension=0, tiled=True),
        lax.psum_scatter(grad_w_down, "item", scatter_dimension=0, tiled=True),
    )
    shard_qkv, shard_out, shard_up, shard_down = lax.psum(
        (shard_qkv, shard_out, shard_up, shard_down), "seq"
    )
    local_squares = (
        jnp.sum(shard_qkv * shard_qkv)
        + jnp.sum(shard_out * shard_out)
        + jnp.sum(shard_up * shard_up)
        + jnp.sum(shard_down * shard_down)
    )
    matrix_squares = lax.psum(local_squares, "item")
    grad_norm = jnp.sqrt(matrix_squares + jnp.sum(small_total * small_total))
    factor = jnp.minimum(1.0, clip_level / (grad_norm + 1e-06))
    new_qkv = adam_update(
        w_qkv, first_qkv, second_qkv, shard_qkv * factor, weight_decay, learn_rate
    )
    new_out = adam_update(
        w_out, first_out, second_out, shard_out * factor, weight_decay, learn_rate
    )
    new_up = adam_update(w_up, first_up, second_up, shard_up * factor, weight_decay, learn_rate)
    new_down = adam_update(
        w_down, first_down, second_down, shard_down * factor, weight_decay, learn_rate
    )
    new_small = adam_update(
        small_params, first_small, second_small, small_total * factor, 0.0, small_rate
    )
    return (
        outputs.astype(bf16).reshape(items_n, tok_rows, width),
        grad_inputs.reshape(items_n, tok_rows, width),
        grad_norm,
        new_qkv[0],
        new_qkv[1],
        new_qkv[2],
        new_out[0],
        new_out[1],
        new_out[2],
        new_up[0],
        new_up[1],
        new_up[2],
        new_down[0],
        new_down[1],
        new_down[2],
        new_small[0],
        new_small[1],
        new_small[2],
    )


def solution(mesh):
    return jax.shard_map(
        on_device,
        mesh=mesh,
        in_specs=(
            P("item", "seq", None),
            P("item", "seq", None),
            P("item"),
            P("item", None),
            P("item", "seq", None, None),
            P("item", None),
            P("item", None),
            P("item", None),
            P("item", None),
            P(),
            P("item", None),
            P("item", None),
            P("item", None),
            P("item", None),
            P("item", None),
            P("item", None),
            P("item", None),
            P("item", None),
            P(),
            P(),
        ),
        out_specs=(
            P("item", "seq", None),
            P("item", "seq", None),
            P(),
            P("item", None),
            P("item", None),
            P("item", None),
            P("item", None),
            P("item", None),
            P("item", None),
            P("item", None),
            P("item", None),
            P("item", None),
            P("item", None),
            P("item", None),
            P("item", None),
            P(),
            P(),
            P(),
        ),
        check_vma=False,
    )
```

profile of v0, /device:TPU:0, one launch (start us, length us, event | category | flops | bytes accessed | tf_op | source)
XLA Modules:
  0.0 2047.1 jit_solution(2048873980352635578)
XLA Ops:
  12.8 65.9 %all-gather.5.cloned.1.call-done = bf16[768,2304]{1,0:T(8,128)(2,1)} async-done(((bf16[96,2304]{1,0:T(8,128)(2,1)}), bf16[768,2304]{1,0:T(8,128)(2,1)}) %all-gather.5.cloned.1.call-update) | async-done | bytes 3538960 | tf_op jit(solution)/shard_map/all_gather | solution.py:198
  100.4 36.2 %all-to-all-done = bf16[1,768,3,4,192]{1,4,2,0,3:T(8,128)(2,1)S(1)} async-done(((bf16[1,768,3,4,192]{1,4,2,0,3:T(8,128)(2,1)}), bf16[1,768,3,4,192]{1,4,2,0,3:T(8,128)(2,1)S(1)}, u32[]{:S(2)}, u32[]{:S(2)}) %all-to-all-start) | async-done | bytes 3538976 | tf_op jit(solution)/shard_map/all_to_all | solution.py:208
  155.4 150.5 %while.129 = (s32[]{:T(128)}, bf16[6,512,64]{1,2,0:T(8,128)(2,1)}, f32[6,512]{1,0:T(8,128)S(1)}, s32[6]{0:T(128)}, pred[48,48]{1,0:T(8,128)(4,1)}, /*index=5*/bf...) while((s32[]{:T(128)}, bf16[6,512,64]{1,2,0:T(8,128)(2,1)}, ...), condition=%wide.region_5.6_spmd, body=%wide.region_2.5_spmd.sunk | while | flops 415268352 | bytes 53303340 | solution.py:73
  313.6 158.1 %while.130 = (s32[]{:T(128)}, bf16[6,512,64]{1,2,0:T(8,128)(2,1)}, f32[6,512]{1,0:T(8,128)}, s32[6]{0:T(128)}, pred[48,48]{1,0:T(8,128)(4,1)}, /*index=5*/bf16[3...) while((s32[]{:T(128)}, bf16[6,512,64]{1,2,0:T(8,128)(2,1)}, ...), condition=%wide.region_9.10_spmd, body=%wide.region_6.9_spmd.sunk | while | flops 415268352 | bytes 53303340 | solution.py:73
  478.8 150.4 %while.131 = (s32[]{:T(128)}, bf16[6,512,64]{1,2,0:T(8,128)(2,1)}, f32[6,512]{1,0:T(8,128)S(1)}, s32[6]{0:T(128)}, pred[48,48]{1,0:T(8,128)(4,1)}, /*index=5*/bf...) while((s32[]{:T(128)}, bf16[6,512,64]{1,2,0:T(8,128)(2,1)}, ...), condition=%wide.region_13.14_spmd, body=%wide.region_10.13_spmd.sunk | while | flops 415268352 | bytes 53303340 | solution.py:73
  640.3 18.3 reduce.19
  669.7 13.1 all-to-all-done.1
  699.3 28.9 %multiply_convert_fusion.3 = (bf16[768,3072]{1,0:T(8,128)(2,1)}, f32[768,3072]{1,0:T(8,128)}, f32[768,3072]{1,0:T(8,128)}) fusion(f32[3072]{0:T(1024)} %add.442, bf16[768,3072]{1,0:T(8,128)(2,1)} %all-gather.9.cloned.1.call-done, f32[768,768]{0,1:T(8,128)S(1)} %get-tuple-element.1667, f32[768]{0:T(1024)} %get-tuple-element.1485, f32[768]{0:T(1024)S(1)} %copy-done.60, ...), kind=kOutput, calls=%fused_computation.100 | convolution fusion | flops 3782541312 | bytes 30695424 | tf_op jit(solution)/shard_map/dot_general | solution.py:228
  741.6 13.4 convert_reduce_fusion
  777.0 10.4 all-to-all-done.2
  791.2 183.6 %while.132 = (s32[]{:T(128)}, f32[3072,64]{0,1:T(8,128)}, f32[3072,64]{0,1:T(8,128)}, bf16[6,512,64]{1,2,0:T(8,128)(2,1)}, s32[6]{0:T(128)}, /*index=5*/pred[48,...) while((s32[]{:T(128)}, f32[3072,64]{0,1:T(8,128)}, ...), condition=%wide.region_24.25_spmd.clone, body=%wide.region_22.24_spmd.clone.sunk | while | flops 1021804032 | bytes 112210064 | solution.py:109
  975.6 179.5 %while.133 = (s32[]{:T(128)}, f32[3072,64]{0,1:T(8,128)}, f32[3072,64]{0,1:T(8,128)}, bf16[6,512,64]{1,2,0:T(8,128)(2,1)}, s32[6]{0:T(128)}, /*index=5*/pred[48,...) while((s32[]{:T(128)}, f32[3072,64]{0,1:T(8,128)}, ...), condition=%wide.region_27.28_spmd.clone, body=%wide.region_25.27_spmd.clone.sunk | while | flops 1021804032 | bytes 112603280 | solution.py:109
  1155.1 180.3 %while.134 = (s32[]{:T(128)}, f32[3072,64]{0,1:T(8,128)}, f32[3072,64]{0,1:T(8,128)}, bf16[6,512,64]{1,2,0:T(8,128)(2,1)S(1)}, s32[6]{0:T(128)}, /*index=5*/pred...) while((s32[]{:T(128)}, f32[3072,64]{0,1:T(8,128)}, ...), condition=%wide.region_30.31_spmd.clone, body=%wide.region_28.30_spmd.clone.sunk | while | flops 1021804032 | bytes 112602776 | solution.py:109
  1350.0 77.3 %all_to_all.60 = bf16[1,3072,3,1,192]{4,2,3,0,1:T(4,128)(2,1)} all-to-all(bf16[1,3072,3,1,192]{4,2,3,0,1:T(4,128)(2,1)} %copy.416), channel_id=1, replica_groups=mesh['item'=8,'seq'=4] {'seq'}, dimensions={1} | all-to-all | bytes 7077888 | tf_op jit(solution)/shard_map/all_to_all | solution.py:263
  1427.4 10.5 copy.427
  1453.4 10.3 fusion.105
  1464.4 10.7 fusion.86
  1475.2 104.8 %reduce-scatter.13.cloned.1.call-done = f32[96,2304]{1,0:T(8,128)} async-done(((f32[768,2304]{1,0:T(8,128)}), f32[96,2304]{1,0:T(8,128)}) %reduce-scatter.13.cloned.1.call-update) | async-done | bytes 884752 | tf_op jit(solution)/shard_map/reduce_scatter | solution.py:288
  1580.0 166.6 %reduce-scatter.11.cloned.1.call-done = f32[384,768]{1,0:T(8,128)} async-done(((f32[3072,768]{1,0:T(8,128)}), f32[384,768]{1,0:T(8,128)}) %reduce-scatter.11.cloned.1.call-update) | async-done | bytes 1179664 | tf_op jit(solution)/shard_map/reduce_scatter | solution.py:291
  1746.6 166.6 %reduce-scatter.9.cloned.1.call-done = f32[96,3072]{1,0:T(8,128)} async-done(((f32[768,3072]{1,0:T(8,128)}), f32[96,3072]{1,0:T(8,128)}) %reduce-scatter.9.cloned.1.call-update) | async-done | bytes 1179664 | tf_op jit(solution)/shard_map/reduce_scatter | solution.py:290
  1925.5 40.7 %psum.47 = f32[12,768]{1,0:T(8,128)S(1)} all-reduce(f32[12,768]{1,0:T(8,128)S(1)} %concatenate.39), channel_id=1, replica_groups=mesh['item'=8,'seq'=4] {'item','seq'}, use_global_device_ids=true, to_apply=%region_52.53 | all-reduce | flops 9216 | bytes 73728 | tf_op jit(solution)/shard_map/psum | solution.py:286
  1966.8 8.1 add_bitcast_fusion
  1975.0 16.8 all-reduce.3.cloned.1.call-done
  2004.4 21.7 %psum.46 = f32[]{:T(128)} all-reduce(f32[]{:T(128)S(6)} %add.457), channel_id=1, replica_groups=mesh['item'=8,'seq'=4] {'item'}, use_global_device_ids=true, to_apply=%region_43.44 | all-reduce | flops 1 | bytes 8 | tf_op jit(solution)/shard_map/psum | solution.py:302
  (852 shorter events, 1062.7 us)
Async XLA Ops:
  7.2 71.5 %copy-start.41 = (bf16[1,768,768]{2,1,0:T(8,128)(2,1)S(1)}, bf16[1,768,768]{2,1,0:T(8,128)(2,1)}, u32[]{:S(2)}) copy-start(bf16[1,768,768]{2,1,0:T(8,128)(2,1)} %param.32) | copy-start | bytes 3538948
  7.2 71.5 %all-gather.5.cloned.1.call-start = ((), (), s32[]{:S(2)}) async-start(), calls=%async_computation.8 | async-start | bytes 3981312 | tf_op jit(solution)/shard_map/all_gather | solution.py:198
  9.4 686.0 %all-gather.7.cloned.1.call-start = ((), (), s32[]{:S(2)}) async-start(), calls=%async_computation.9 | async-start | bytes 1327104 | tf_op jit(solution)/shard_map/all_gather | solution.py:199
  11.1 687.9 %all-gather.9.cloned.1.call-start = ((), (), s32[]{:S(2)}) async-start(), calls=%async_computation.10 | async-start | bytes 5308416 | tf_op jit(solution)/shard_map/all_gather | solution.py:200
  91.7 44.9 %all-to-all-start = ((bf16[1,768,3,4,192]{1,4,2,0,3:T(8,128)(2,1)}), bf16[1,768,3,4,192]{1,4,2,0,3:T(8,128)(2,1)S(1)}, u32[]{:S(2)}, u32[]{:S(2)}) async-start(bf16[1,768,3,4,192]{1,4,2,0,3:T(8,128)(2,1)} %copy.380), calls=%async_computation | async-start | bytes 7077888 | tf_op jit(solution)/shard_map/all_to_all | solution.py:208
  95.5 632.7 %all-gather.11.cloned.1.call-start = ((), (), s32[]{:S(2)}) async-start(), calls=%async_computation.11 | async-start | bytes 5308416 | tf_op jit(solution)/shard_map/all_gather | solution.py:201
  155.4 154.5 %copy-start.35 = (bf16[3072,64]{0,1:T(8,128)(2,1)S(1)}, bf16[3072,64]{0,1:T(8,128)(2,1)}, u32[]{:S(2)}) copy-start(bf16[3072,64]{0,1:T(8,128)(2,1)} %get-tuple-element.1651) | copy-start | bytes 1179652
  313.5 162.1 %copy-start.32 = (bf16[3072,64]{0,1:T(8,128)(2,1)S(1)}, bf16[3072,64]{0,1:T(8,128)(2,1)}, u32[]{:S(2)}) copy-start(bf16[3072,64]{0,1:T(8,128)(2,1)} %get-tuple-element.1648) | copy-start | bytes 1179652
  478.8 151.4 %copy-start.33 = (bf16[6,8,8,512]{3,2,0,1:T(8,128)(2,1)S(1)}, bf16[6,8,8,512]{3,2,0,1:T(8,128)(2,1)}, u32[]{:S(2)}) copy-start(bf16[6,8,8,512]{3,2,0,1:T(8,128)(2,1)} %copy.434) | copy-start | bytes 1179652
  663.1 19.7 all-to-all-start.1
  669.7 85.4 %copy-start.14 = (bf16[1,768,768]{1,2,0:T(8,128)(2,1)}, bf16[1,768,768]{1,2,0:T(8,128)(2,1)S(1)}, u32[]{:S(2)}) copy-start(bf16[1,768,768]{1,2,0:T(8,128)(2,1)S(1)} %copy.397) | copy-start | bytes 3538948
  698.6 64.4 %copy-start.22 = (f32[768,768]{0,1:T(8,128)}, f32[768,768]{0,1:T(8,128)S(1)}, u32[]{:S(2)}) copy-start(f32[768,768]{0,1:T(8,128)S(1)} %get-tuple-element.1667) | copy-start | bytes 7077892
  698.7 64.3 %copy-start.58 = (f32[768]{0:T(1024)}, f32[768]{0:T(1024)S(1)}, u32[]{:S(2)}) copy-start(f32[768]{0:T(1024)S(1)} %broadcast_multiply_fusion.1) | copy-start | bytes 9220
  699.0 64.0 %copy-start.67 = (f32[768]{0:T(1024)}, f32[768]{0:T(1024)S(1)}, u32[]{:S(2)}) copy-start(f32[768]{0:T(1024)S(1)} %fusion.82) | copy-start | bytes 9220
  738.8 16.2 slice-start.1
  767.9 19.5 all-to-all-start.2
  771.6 703.6 %reduce-scatter.7.cloned.1.call-start = ((), (), s32[]{:S(2)}) async-start(), calls=%async_computation.12 | async-start | bytes 2654208 | tf_op jit(solution)/shard_map/reduce_scatter | solution.py:289
  776.9 803.1 %reduce-scatter.13.cloned.1.call-start = ((), (), s32[]{:S(2)}) async-start(), calls=%async_computation.15 | async-start | bytes 7962624 | tf_op jit(solution)/shard_map/reduce_scatter | solution.py:288
  1453.2 293.4 %reduce-scatter.11.cloned.1.call-start = ((), (), s32[]{:S(2)}) async-start(), calls=%async_computation.14 | async-start | bytes 10616832 | tf_op jit(solution)/shard_map/reduce_scatter | solution.py:291
  1463.7 449.5 %reduce-scatter.9.cloned.1.call-start = ((), (), s32[]{:S(2)}) async-start(), calls=%async_computation.13 | async-start | bytes 10616832 | tf_op jit(solution)/shard_map/reduce_scatter | solution.py:290
  1475.1 516.7 %all-reduce.3.cloned.1.call-start = ((), (), s32[]{:S(2)}) async-start(), calls=%async_computation.16 | async-start | bytes 7077888 | tf_op jit(solution)/shard_map/psum | solution.py:293
  1922.8 44.1 %copy-start.66 = (f32[768]{0:T(1024)S(1)}, f32[768]{0:T(1024)}, u32[]{:S(2)}) copy-start(f32[768]{0:T(1024)} %copy-done.65) | copy-start | bytes 9220
  2001.2 27.8 %copy-start.23 = (f32[384,768]{1,0:T(8,128)S(1)}, f32[384,768]{1,0:T(8,128)}, u32[]{:S(2)}) copy-start(f32[384,768]{1,0:T(8,128)} %param.40) | copy-start | bytes 3538948
  2001.2 27.8 %copy-start.45 = (f32[384,768]{1,0:T(8,128)S(1)}, f32[384,768]{1,0:T(8,128)}, u32[]{:S(2)}) copy-start(f32[384,768]{1,0:T(8,128)} %param.48) | copy-start | bytes 3538948
  (158 other events, 562.3 us)
Sparse Core Ops, SparseCore 0:
  10.8 67.8 all-gather.4
  81.5 39.5 all-gather.6
  123.8 78.6 all-gather.8
  205.1 78.0 all-gather.10
  777.1 67.8 reduce-scatter.6
  1453.3 126.6 reduce-scatter.12
  1584.0 162.4 reduce-scatter.10
  1750.6 162.5 reduce-scatter.8
  1916.0 75.7 all-reduce.2
where the time goes:
time: 2060 us; the launch traced here: 2050 us
  waiting for transfers between devices  581 us (28%)
  local copies, waits for them, and re-layouts  566 us (27%)
  matrix products  474 us (23%)
  loops' own time  143 us (7%)
  blocking collectives  140 us (7%)
  other arithmetic  111 us (5%)
  between operations  20.7 us (1%)
    broadcast_in_dim x72, local copies, waits for them, and re-layouts, masked_scores(): shaped = jnp.where(allowed_rows[:, None, :, None], shaped, masked_value)  312 us
    reduce_scatter x1, waiting for transfers between devices, on_device(): lax.psum_scatter(grad_w_up, 'item', scatter_dimension=0, tiled=True)  167 us
    reduce_scatter x1, waiting for transfers between devices, on_device(): lax.psum_scatter(grad_w_down, 'item', scatter_dimension=0, tiled=True)  167 us
    dot_general x36, matrix products, masked_scores(): jnp.einsum('qd,kd->qk', q_block, k_head, preferred_element_type=jnp.float32)  117 us
    reduce_scatter x1, waiting for transfers between devices, on_device(): lax.psum_scatter(grad_w_qkv, 'item', scatter_dimension=0, tiled=True)  105 us
    dot_general x18, matrix products, rows_forward(): mixed = jnp.dot(attn_prob, v_head, preferred_element_type=jnp.float32)  85.9 us
    all_to_all x1, blocking collectives, on_device(): lax.all_to_all(shortened(grad_qkv_heads), 'seq', split_axis=1, concat_axi...  77.3 us
    another operation x3, loops' own time, head_backward(): lax.scan(rows_backward, (zero_rows, zero_rows), offsets)  72.3 us
  transfers between devices with their start and end apart: 12, of which 8 were waited for; matrix products, arithmetic and copies ran while one was open for 51% of the time, Pallas kernels for 0%

commit v1 on v0

v1 whole, which is shorter than its diff:
```python
import functools

import jax
import jax.numpy as jnp
from jax import lax
from jax.experimental import pallas as pl
from jax.experimental.pallas import tpu as pltpu
from jax.sharding import PartitionSpec as P

ADAM_STEP = 10
norm_epsilon = 1e-06
beta_first = 0.9
beta_second = 0.999
adam_epsilon = 1e-08
learn_rate = 0.1
small_rate = 0.5
weight_decay = 0.01
clip_level = 1.0


HD=64; BL=64; NEG=-1e30
bf16=jnp.bfloat16; f32=jnp.float32
NT=(((1,),(1,)),((),()))
TN=(((0,),(0,)),((),()))

def slots(count, positions, table):
    H,NB,R=table.shape; G=positions.shape[0]
    a=jnp.arange(NB,dtype=jnp.int32)
    win=jnp.stack([a-1,a,a+1],-1)
    act=jnp.arange(G,dtype=jnp.int32)<count
    parts=jnp.concatenate([jnp.broadcast_to(win[None],(H,NB,3)),
        jnp.broadcast_to(jnp.where(act,positions,-1)[None,None],(H,NB,G)),table],-1)
    S=3+G+R
    ok=(parts>=0)&(parts<NB)
    same=parts[...,:,None]==parts[...,None,:]
    earlier=jnp.arange(S)[:,None]>jnp.arange(S)[None,:]
    dup=jnp.any(same&earlier,-1)
    isg=jnp.any((positions[None,:]==a[:,None])&act[None],-1)
    ok=ok&~dup&~isg[None,:,None]
    idx=jnp.clip(parts,0,NB-1)
    bias=jnp.where(ok,0.0,NEG).astype(f32)
    bias=jnp.broadcast_to(bias[...,None],(H,NB,S,BL)).reshape(H*NB,S*BL)
    return idx.reshape(-1), bias

def lo_lanes(rows):
    return lax.broadcasted_iota(jnp.int32,(rows,2*HD),1)<HD

def pick(block,h,which):
    low=lo_lanes(block.shape[0])
    keep_low=(h%2==1) if which=='q' else (h%2==0)
    return jnp.where(low if keep_low else ~low, block, jnp.zeros_like(block))

def fwd_kernel(H,NB,S,G,CH,idx_ref,gl_ref,qkv_ref,bias_ref,out_ref,lse_ref,sbuf):
    n=NB*BL
    def finish(r,outs,lses):
        low=lo_lanes(BL)
        for p in range((H+1)//2):
            if 2*p+1<H:
                out_ref[pl.ds(r,BL),p*128:(p+1)*128]=jnp.where(low,outs[2*p],outs[2*p+1]).astype(bf16)
            else:
                out_ref[pl.ds(r,BL),p*128:p*128+HD]=outs[2*p][:,:HD].astype(bf16)
        lane=lax.broadcasted_iota(jnp.int32,(BL,128),1)
        acc=jnp.zeros((BL,128),f32)
        for h in range(H): acc=jnp.where(lane==h,lses[h],acc)
        lse_ref[pl.ds(r,BL),:]=acc
    def qblk(r,h):
        return pick(qkv_ref[pl.ds(r,BL),(H+h//2)*128:(H+h//2+1)*128],h,'q')
    def body(a,_):
        r=pl.multiple_of(a*BL,BL)
        outs=[];lses=[]
        for h in range(H):
            kv=jnp.concatenate([qkv_ref[pl.ds(pl.multiple_of(idx_ref[(h*NB+a)*S+j]*BL,BL),BL),h*128:(h+1)*128] for j in range(S)],0)
            s=lax.dot_general(qblk(r,h),kv,NT,preferred_element_type=f32)+bias_ref[pl.ds(h*NB+a,1),:]
            m=jnp.max(s,-1,keepdims=True)
            e=jnp.exp(s-m)
            l=jnp.sum(e,-1,keepdims=True)
            p=(e*(1.0/l)).astype(bf16)
            outs.append(jnp.dot(p,kv,preferred_element_type=f32))
            lses.append(m+jnp.log(l))
        finish(r,outs,lses)
        return 0
    lax.fori_loop(0,NB,body,0,unroll=UNROLL)
    def gbody(g,_):
        r=pl.multiple_of(gl_ref[1+g]*BL,BL)
        outs=[];lses=[]
        for h in range(H):
            q=qblk(r,h)
            mm=None
            for c in range(n//CH):
                s=lax.dot_general(q,qkv_ref[c*CH:(c+1)*CH,h*128:(h+1)*128],NT,preferred_element_type=f32)
                sbuf[h,:,c*CH:(c+1)*CH]=s
                mc=jnp.max(s,-1,keepdims=True)
                mm=mc if mm is None else jnp.maximum(mm,mc)
            l=0.;
            for c in range(n//CH):
                e=jnp.exp(sbuf[h,:,c*CH:(c+1)*CH]-mm)
                sbuf[h,:,c*CH:(c+1)*CH]=e
                l=l+jnp.sum(e,-1,keepdims=True)
            il=1.0/l
            o=0.
            for c in range(n//CH):
                p=(sbuf[h,:,c*CH:(c+1)*CH]*il).astype(bf16)
                o=o+jnp.dot(p,qkv_ref[c*CH:(c+1)*CH,h*128:(h+1)*128],preferred_element_type=f32)
            outs.append(o); lses.append(mm+jnp.log(l))
        finish(r,outs,lses)
        return 0
    lax.fori_loop(0,gl_ref[0],gbody,0)
UNROLL=1
def attn_fwd(idx,gl,qkv,bias,H,NB,S):
    n=NB*BL
    V=pl.BlockSpec(memory_space=pltpu.VMEM); SM=pl.BlockSpec(memory_space=pltpu.SMEM)
    return pl.pallas_call(functools.partial(fwd_kernel,H,NB,S,0,512),
        out_shape=(jax.ShapeDtypeStruct((n,H*HD),bf16),jax.ShapeDtypeStruct((n,128),f32)),
        in_specs=[SM,SM,V,V],out_specs=(V,V),
        scratch_shapes=[pltpu.VMEM((H,BL,n),f32)],
        compiler_params=pltpu.CompilerParams(vmem_limit_bytes=56<<20),name="attn_fwd")(idx,gl,qkv,bias)

def bwd_kernel(H,NB,S,CH,idx_ref,gl_ref,qkv_ref,g_ref,lse_ref,bias_ref,out_ref,acc,pbuf,dbuf):
    n=NB*BL
    QP=(H+1)//2
    def zero(i,_):
        acc[pl.ds(pl.multiple_of(i*256,256),256),:]=jnp.zeros((256,H*128),f32)
        return 0
    lax.fori_loop(0,n//256,zero,0)
    def xblk(r,h):
        q=pick(qkv_ref[pl.ds(r,BL),(H+h//2)*128:(H+h//2+1)*128],h,'q')
        w=min(128,H*HD-(h//2)*128)
        g=g_ref[pl.ds(r,BL),(h//2)*128:(h//2)*128+w]
        if w<128: g=jnp.concatenate([g,jnp.zeros((BL,128-w),bf16)],1)
        else: g=pick(g,h,'g')
        return jnp.concatenate([q,g],0)
    def finish(r,dqs):
        low=lo_lanes(BL)
        for p in range(QP):
            hi=dqs[2*p]; lo=dqs[2*p+1] if 2*p+1<H else jnp.zeros_like(hi)
            out_ref[pl.ds(r,BL),(H+p)*128:(H+p+1)*128]=jnp.where(low,lo,hi).astype(bf16)
    def body(a,_):
        r=pl.multiple_of(a*BL,BL)
        dqs=[]
        for h in range(H):
            x=xblk(r,h)
            rows=[pl.multiple_of(idx_ref[(h*NB+a)*S+j]*BL,BL) for j in range(S)]
            kv=jnp.concatenate([qkv_ref[pl.ds(rows[j],BL),h*128:(h+1)*128] for j in range(S)],0)
            sd=lax.dot_general(x,kv,NT,preferred_element_type=f32)
            p=jnp.exp(sd[:BL]+bias_ref[pl.ds(h*NB+a,1),:]-lse_ref[pl.ds(r,BL),h:h+1])
            dp=sd[BL:]
            inner=jnp.sum(dp*p,-1,keepdims=True)
            ds=p*(dp-inner)
            w=jnp.concatenate([ds.astype(bf16),p.astype(bf16)],0)
            dqs.append(jnp.dot(w[:BL],kv,preferred_element_type=f32))
            dkv=lax.dot_general(w,x,TN,preferred_element_type=f32)
            for j in range(S):
                acc[pl.ds(rows[j],BL),h*128:(h+1)*128]+=dkv[j*BL:(j+1)*BL]
        finish(r,dqs)
        return 0
    lax.fori_loop(0,NB,body,0,unroll=UNROLL)
    def gbody(g,_):
        r=pl.multiple_of(gl_ref[1+g]*BL,BL)
        dqs=[]
        for h in range(H):
            x=xblk(r,h)
            lse=lse_ref[pl.ds(r,BL),h:h+1]
            inner=0.
            for c in range(n//CH):
                cs=slice(c*CH,(c+1)*CH)
                sd=lax.dot_general(x,qkv_ref[cs,h*128:(h+1)*128],NT,preferred_element_type=f32)
                p=jnp.exp(sd[:BL]-lse); dp=sd[BL:]
                pbuf[h,:,cs]=p; dbuf[h,:,cs]=dp
                inner=inner+jnp.sum(dp*p,-1,keepdims=True)
            dq=0.
            for c in range(n//CH):
                cs=slice(c*CH,(c+1)*CH)
                p=pbuf[h,:,cs]
                ds=(p*(dbuf[h,:,cs]-inner)).astype(bf16)
                w=jnp.concatenate([ds,p.astype(bf16)],0)
                dq=dq+jnp.dot(ds,qkv_ref[cs,h*128:(h+1)*128],preferred_element_type=f32)
                acc[cs,h*128:(h+1)*128]+=lax.dot_general(w,x,TN,preferred_element_type=f32)
            dqs.append(dq)
        finish(r,dqs)
        return 0
    lax.fori_loop(0,gl_ref[0],gbody,0)
    def flush(i,_):
        rr=pl.ds(pl.multiple_of(i*256,256),256)
        out_ref[rr,:H*128]=acc[rr,:].astype(bf16)
        return 0
    lax.fori_loop(0,n//256,flush,0)

def attn_bwd(idx,gl,qkv,g,lse,bias,H,NB,S):
    n=NB*BL
    V=pl.BlockSpec(memory_space=pltpu.VMEM); SM=pl.BlockSpec(memory_space=pltpu.SMEM)
    return pl.pallas_call(functools.partial(bwd_kernel,H,NB,S,512),
        out_shape=jax.ShapeDtypeStruct((n,(H+(H+1)//2)*128),bf16),
        in_specs=[SM,SM,V,V,V,V],out_specs=V,
        scratch_shapes=[pltpu.VMEM((n,H*128),f32),pltpu.VMEM((H,BL,n),f32),pltpu.VMEM((H,BL,n),f32)],
        compiler_params=pltpu.CompilerParams(vmem_limit_bytes=56<<20),name="attn_bwd")(idx,gl,qkv,g,lse,bias)


def layer_norm(values, gain, bias):
    average = jnp.mean(values, -1, keepdims=True)
    centered = values - average
    spread = jnp.mean(centered * centered, -1, keepdims=True)
    return centered * lax.rsqrt(spread + norm_epsilon) * gain + bias


def exact_gelu(values):
    return jax.nn.gelu(values, approximate=False)


def packed_columns(own):
    heads = own.shape[2]
    cols = []
    for h in range(heads):
        pair = [own[:, 2, h], own[:, 1, h]]
        cols += pair if h % 2 == 0 else pair[::-1]
    for p in range((heads + 1) // 2):
        odd = own[:, 0, 2 * p + 1] if 2 * p + 1 < heads else jnp.zeros_like(own[:, 0, 0])
        cols += [odd * HD**-0.5, own[:, 0, 2 * p] * HD**-0.5]
    return jnp.concatenate(cols, -1)


def natural_columns(values, heads):
    parts = [[], [], []]
    for h in range(heads):
        first, second = values[:, h * 128 : h * 128 + HD], values[:, h * 128 + HD : h * 128 + 128]
        base = (heads + h // 2) * 128
        if h % 2 == 0:
            parts[2].append(first)
            parts[1].append(second)
            parts[0].append(values[:, base + HD : base + 128] * HD**-0.5)
        else:
            parts[1].append(first)
            parts[2].append(second)
            parts[0].append(values[:, base : base + HD] * HD**-0.5)
    return jnp.concatenate(parts[0] + parts[1] + parts[2], -1)


def adam_update(weight, first, second, grad, decay, rate):
    first_new = beta_first * first + (1.0 - beta_first) * grad
    second_new = beta_second * second + (1.0 - beta_second) * grad * grad
    first_hat = first_new / (1.0 - beta_first**ADAM_STEP)
    second_hat = second_new / (1.0 - beta_second**ADAM_STEP)
    weight_new = weight - rate * (
        first_hat / (jnp.sqrt(second_hat) + adam_epsilon) + decay * weight
    )
    return (weight_new, first_new, second_new)


def on_device(
    inputs,
    d_output,
    glob_count,
    glob_pos,
    rand_blocks,
    w_qkv,
    w_out,
    w_up,
    w_down,
    small_params,
    first_qkv,
    second_qkv,
    first_out,
    second_out,
    first_up,
    second_up,
    first_down,
    second_down,
    first_small,
    second_small,
):
    items_n, tok_rows, width = inputs.shape
    groups = lax.axis_size("seq")
    place = lax.axis_index("seq")
    heads = rand_blocks.shape[1]
    nblocks = rand_blocks.shape[2]
    head_width = heads * HD
    positions_n = tok_rows * groups
    row_count = tok_rows
    slots_n = 3 + glob_pos.shape[1] + rand_blocks.shape[3]

    own = lax.dynamic_index_in_dim(
        w_qkv.reshape(-1, 3, groups, heads, HD), place, 2, keepdims=False
    )
    slab = lax.all_gather(packed_columns(own).astype(bf16), "item", axis=0, tiled=True)
    full_out, full_up, full_down = (
        lax.all_gather(w_out.astype(bf16), "item", axis=0, tiled=True),
        lax.all_gather(w_up.astype(bf16), "item", axis=0, tiled=True),
        lax.all_gather(w_down.astype(bf16), "item", axis=0, tiled=True),
    )
    bias3 = jnp.stack([small_params[2], jnp.zeros((width,), f32), small_params[3]])
    own_bias = lax.dynamic_index_in_dim(
        bias3.reshape(1, 3, groups, heads, HD), place, 2, keepdims=False
    )
    slab_bias = packed_columns(own_bias)
    tokens_b = inputs.reshape(tok_rows, width)
    tokens_all = lax.all_gather(tokens_b, "seq", axis=0, tiled=True)
    tokens_f = tokens_b.astype(f32)
    qkv = (jnp.dot(tokens_all, slab, preferred_element_type=f32) + slab_bias).astype(bf16)
    idx, bias = slots(glob_count[0], glob_pos[0], rand_blocks[0])
    gl = jnp.concatenate([glob_count, glob_pos[0]])
    mixed_heads, lse = attn_fwd(idx, gl, qkv, bias, heads, nblocks, slots_n)
    mixed = lax.all_to_all(mixed_heads, "seq", split_axis=0, concat_axis=1, tiled=True)
    attn_out = jnp.dot(mixed, full_out, preferred_element_type=f32) + small_params[4]
    hidden, norm_one_back = jax.vjp(
        layer_norm, tokens_f + attn_out, small_params[0], small_params[1]
    )
    hidden_b = hidden.astype(bf16)
    up_pre = jnp.dot(hidden_b, full_up, preferred_element_type=f32) + small_params[8:12].reshape(-1)
    active, gelu_back = jax.vjp(exact_gelu, up_pre)
    active_b = active.astype(bf16)
    ffn_out = jnp.dot(active_b, full_down, preferred_element_type=f32) + small_params[7]
    outputs, norm_two_back = jax.vjp(layer_norm, hidden + ffn_out, small_params[5], small_params[6])
    grad_second, grad_gain_two, grad_bias_two = norm_two_back(
        d_output.reshape(row_count, width).astype(f32)
    )
    grad_ffn = grad_second.astype(bf16)
    grad_w_down = jnp.einsum("rf,rd->fd", active_b, grad_ffn, preferred_element_type=f32)
    grad_active = jnp.einsum("rd,fd->rf", grad_ffn, full_down, preferred_element_type=f32)
    (grad_up_pre,) = gelu_back(grad_active)
    grad_up_b = grad_up_pre.astype(bf16)
    grad_w_up = jnp.einsum("rd,rf->df", hidden_b, grad_up_b, preferred_element_type=f32)
    grad_hidden = grad_second + jnp.einsum(
        "rf,df->rd", grad_up_b, full_up, preferred_element_type=f32
    )
    grad_first, grad_gain_one, grad_bias_one = norm_one_back(grad_hidden)
    grad_attn = grad_first.astype(bf16)
    grad_w_out = jnp.einsum("rm,rd->md", mixed, grad_attn, preferred_element_type=f32)
    grad_mixed = jnp.einsum("rd,md->rm", grad_attn, full_out, preferred_element_type=f32).astype(
        bf16
    )
    grad_heads = lax.all_to_all(grad_mixed, "seq", split_axis=1, concat_axis=0, tiled=True)
    grad_qkv = attn_bwd(idx, gl, qkv, grad_heads, lse, bias, heads, nblocks, slots_n)
    grad_slab = jnp.einsum("rd,re->de", tokens_all, grad_qkv, preferred_element_type=f32)
    grad_tokens = jnp.einsum("re,de->rd", grad_qkv, slab, preferred_element_type=f32).astype(bf16)
    grad_inputs = grad_first + lax.psum_scatter(
        grad_tokens, "seq", scatter_dimension=0, tiled=True
    ).astype(f32)
    slab_sum = natural_columns(jnp.sum(grad_qkv.astype(f32), 0)[None], heads)[0]
    bias_grads = lax.dynamic_update_index_in_dim(
        jnp.zeros((3, groups, heads * HD), f32), slab_sum.reshape(3, heads * HD), place, 1
    ).reshape(3, width)
    small_rows = jnp.stack(
        [
            grad_gain_one,
            grad_bias_one,
            bias_grads[0],
            bias_grads[2],
            jnp.sum(grad_attn.astype(f32), 0),
            grad_gain_two,
            grad_bias_two,
            jnp.sum(grad_ffn.astype(f32), 0),
        ]
    )
    small_part = jnp.concatenate(
        [small_rows, jnp.sum(grad_up_b.astype(f32), 0).reshape(4, width)], 0
    )
    small_total = lax.psum(small_part, ("item", "seq"))
    shard_down = lax.psum_scatter(grad_w_down.astype(bf16), "item", scatter_dimension=0, tiled=True)
    shard_up = lax.psum_scatter(grad_w_up.astype(bf16), "item", scatter_dimension=0, tiled=True)
    shard_out = lax.psum_scatter(grad_w_out.astype(bf16), "item", scatter_dimension=0, tiled=True)
    shard_slab = lax.psum_scatter(grad_slab.astype(bf16), "item", scatter_dimension=0, tiled=True)
    shard_slab = natural_columns(shard_slab.astype(f32), heads).reshape(-1, 3, 1, heads * HD)
    shard_qkv = lax.all_gather(shard_slab, "seq", axis=2, tiled=True).reshape(-1, 3 * width)
    shard_out, shard_up, shard_down = lax.psum(
        (shard_out.astype(f32), shard_up.astype(f32), shard_down.astype(f32)), "seq"
    )
    local_squares = (
        jnp.sum(shard_qkv * shard_qkv)
        + jnp.sum(shard_out * shard_out)
        + jnp.sum(shard_up * shard_up)
        + jnp.sum(shard_down * shard_down)
    )
    matrix_squares = lax.psum(local_squares, "item")
    grad_norm = jnp.sqrt(matrix_squares + jnp.sum(small_total * small_total))
    factor = jnp.minimum(1.0, clip_level / (grad_norm + 1e-06))
    new_qkv = adam_update(
        w_qkv, first_qkv, second_qkv, shard_qkv * factor, weight_decay, learn_rate
    )
    new_out = adam_update(
        w_out, first_out, second_out, shard_out * factor, weight_decay, learn_rate
    )
    new_up = adam_update(w_up, first_up, second_up, shard_up * factor, weight_decay, learn_rate)
    new_down = adam_update(
        w_down, first_down, second_down, shard_down * factor, weight_decay, learn_rate
    )
    new_small = adam_update(
        small_params, first_small, second_small, small_total * factor, 0.0, small_rate
    )
    return (
        outputs.astype(bf16).reshape(items_n, tok_rows, width),
        grad_inputs.reshape(items_n, tok_rows, width),
        grad_norm,
        new_qkv[0],
        new_qkv[1],
        new_qkv[2],
        new_out[0],
        new_out[1],
        new_out[2],
        new_up[0],
        new_up[1],
        new_up[2],
        new_down[0],
        new_down[1],
        new_down[2],
        new_small[0],
        new_small[1],
        new_small[2],
    )


def solution(mesh):
    return jax.shard_map(
        on_device,
        mesh=mesh,
        in_specs=(
            P("item", "seq", None),
            P("item", "seq", None),
            P("item"),
            P("item", None),
            P("item", "seq", None, None),
            P("item", None),
            P("item", None),
            P("item", None),
            P("item", None),
            P(),
            P("item", None),
            P("item", None),
            P("item", None),
            P("item", None),
            P("item", None),
            P("item", None),
            P("item", None),
            P("item", None),
            P(),
            P(),
        ),
        out_specs=(
            P("item", "seq", None),
            P("item", "seq", None),
            P(),
            P("item", None),
            P("item", None),
            P("item", None),
            P("item", None),
            P("item", None),
            P("item", None),
            P("item", None),
            P("item", None),
            P("item", None),
            P("item", None),
            P("item", None),
            P("item", None),
            P(),
            P(),
            P(),
        ),
        check_vma=False,
    )
```

time: 2060 us -> 818 us (0.40)
  local copies, waits for them, and re-layouts: 566 us -> 29.4 us
  matrix products: 474 us -> 110 us
  waiting for transfers between devices: 581 us -> 248 us
  Pallas kernels: 0 us -> 153 us
  loops' own time: 143 us -> 0 us
  other arithmetic: 111 us -> 41.1 us
  blocking collectives: 140 us -> 202 us
    dot_general x129 -> x3, matrix products: 387 us -> 24.3 us  [the longest x1 8.48 us: on_device(): jnp.einsum('re,de->rd', grad_qkv, slab, preferred_element_type=f32)]
    broadcast_in_dim x73 -> x5, local copies, waits for them, and re-layouts: 312 us -> 0.45 us  [the longest x1 0.36 us: slots(): jnp.broadcast_to(bias[..., None], (H, NB, S, BL)).reshape(H * NB, S * BL)]
    reduce_scatter x4, waiting for transfers between devices: 438 us -> 169 us  [the longest x1 99.1 us: on_device(): lax.psum_scatter(grad_w_up.astype(bf16), 'item', scatter_dimension=0, til...]
    pallas_call x0 -> x2, Pallas kernels: none -> 153 us  [the longest x1 77.8 us: attn_bwd(): pl.pallas_call(functools.partial(bwd_kernel, H, NB, S, 512), out_shape=ja...]
    another operation x6 -> x0, loops' own time: 143 us -> none  [the longest x3 72.3 us: head_backward(): lax.scan(rows_backward, (zero_rows, zero_rows), offsets)]
    dynamic_slice x90 -> x0, local copies, waits for them, and re-layouts: 79.3 us -> none  [the longest x36 44.6 us: head_forward(): mixed, log_total = lax.map(rows_forward, offsets)]
    psum x0 -> x1, blocking collectives: none -> 75.1 us  [on_device(): lax.psum((shard_out.astype(f32), shard_up.astype(f32), shard_down.astype(...]
    all_gather x1, waiting for transfers between devices: 65.9 us -> 0.02 us  [on_device(): tokens_all = lax.all_gather(tokens_b, 'seq', axis=0, tiled=True)]
  transfers between devices with their start and end apart: 12 -> 10, of which waited for: 8 -> 5; matrix products, arithmetic and copies ran while one was open for 51% -> 16% of each run, Pallas kernels for 0% -> 19%
where the time goes in v1:
time: 818 us; the launch traced here: 810 us
  waiting for transfers between devices  248 us (30%)
  blocking collectives  202 us (25%)
  Pallas kernels  153 us (19%)
  matrix products  110 us (13%)
  other arithmetic  41.1 us (5%)
  local copies, waits for them, and re-layouts  29.4 us (4%)
  between operations  20.8 us (3%)
    reduce_scatter x1, waiting for transfers between devices, on_device(): lax.psum_scatter(grad_w_up.astype(bf16), 'item', scatter_dimension=0, til...  99.1 us
    pallas_call x1, Pallas kernels, attn_bwd(): pl.pallas_call(functools.partial(bwd_kernel, H, NB, S, 512), out_shape=ja...  77.8 us
    pallas_call x1, Pallas kernels, attn_fwd(): pl.pallas_call(functools.partial(fwd_kernel, H, NB, S, 0, 512), out_shape...  75.5 us
    psum x1, blocking collectives, on_device(): lax.psum((shard_out.astype(f32), shard_up.astype(f32), shard_down.astype(...  75.1 us
    reduce_scatter x1, waiting for transfers between devices, on_device(): lax.psum_scatter(grad_w_down.astype(bf16), 'item', scatter_dimension=0, t...  70.3 us
    all_gather x1, waiting for transfers between devices, on_device(): lax.all_gather(w_down.astype(bf16), 'item', axis=0, tiled=True)  51.8 us
    psum x1, blocking collectives, on_device(): small_total = lax.psum(small_part, ('item', 'seq'))  41.1 us
    all_gather x1, blocking collectives, on_device(): lax.all_gather(packed_columns(own).astype(bf16), 'item', axis=0, tiled=True)  34.5 us
  transfers between devices with their start and end apart: 10, of which 5 were waited for; matrix products, arithmetic and copies ran while one was open for 16% of the time, Pallas kernels for 19%

profile of v1, /device:TPU:0, one launch (start us, length us, event | category | flops | bytes accessed | tf_op | source)
XLA Modules:
  0.0 809.9 jit_solution(8067901429611979205)
XLA Ops:
  13.3 34.5 %all_gather.18 = bf16[768,640]{1,0:T(8,128)(2,1)S(1)} all-gather(bf16[96,640]{1,0:T(8,128)(2,1)S(1)} %copy.101), channel_id=1, replica_groups=mesh['item'=8,'seq'=4] {'item'}, dimensions={0}, use_global_device_ids=true | all-gather | bytes 1105920 | tf_op jit(solution)/shard_map/all_gather | solution.py:283
  52.1 8.0 fusion.9.qkv_ref
  60.2 75.5 %attn_fwd.1 = (bf16[3072,192]{1,0:T(8,128)(2,1)}, f32[3072,128]{1,0:T(8,128)}) custom-call(s32[1440]{0:T(1024)} %min.15.idx_ref, s32[5]{0:T(128)} %pad_add_fusion.2.gl_ref, bf16[3072,640]{1,0:T(8,128)(2,1)} %fusion.9.qkv_ref, f32[144,640]{1,0:T(8,128)} %reshape.286.bias_ref), custom_call_target="tpu_custom_call" | custom-call | tf_op jit(solution)/shard_map/attn_fwd/pallas_call | solution.py:112
  138.2 4.4 all-to-all-start
  145.6 12.9 %all-to-all-done = bf16[4,768,192]{1,2,0:T(8,128)(2,1)} async-done(((bf16[4,768,192]{1,2,0:T(8,128)(2,1)}), bf16[4,768,192]{1,2,0:T(8,128)(2,1)}, u32[]{:S(2)}, u32[]{:S(2)}) %all-to-all-start) | async-done | bytes 1179680 | tf_op jit(solution)/shard_map/all_to_all | solution.py:301
  162.9 12.8 %all-gather.8.cloned.1.call-done = bf16[768,3072]{1,0:T(8,128)(2,1)} async-done(((bf16[96,3072]{1,0:T(8,128)(2,1)}), bf16[768,3072]{1,0:T(8,128)(2,1)}) %all-gather.8.cloned.1.call-update) | async-done | bytes 4718608 | tf_op jit(solution)/shard_map/all_gather | solution.py:286
  175.7 28.8 %multiply_convert_fusion = (bf16[768,3072]{1,0:T(8,128)(2,1)}, f32[768,3072]{1,0:T(8,128)}, f32[768,3072]{1,0:T(8,128)}) fusion(f32[3072]{0:T(1024)} %add.242, bf16[768,3072]{1,0:T(8,128)(2,1)} %all-gather.8.cloned.1.call-done, f32[768,768]{0,1:T(8,128)S(1)} %get-tuple-element.181, f32[768]{0:T(1024)} %get-tuple-element.121, ...), kind=kOutput, calls=%fused_computation.4 | convolution fusion | flops 3782541312 | bytes 30695424 | tf_op jit(solution)/shard_map/dot_general | solution.py:307
  204.6 51.8 %all-gather.10.cloned.1.call-done = bf16[3072,768]{1,0:T(8,128)(2,1)} async-done(((bf16[384,768]{1,0:T(8,128)(2,1)}), bf16[3072,768]{1,0:T(8,128)(2,1)}) %all-gather.10.cloned.1.call-update) | async-done | bytes 4718608 | tf_op jit(solution)/shard_map/all_gather | solution.py:287
  256.4 8.1 fusion.60
  269.8 13.6 %convert_reduce_fusion = (f32[3072]{0:T(1024)}, bf16[768,3072]{1,0:T(8,128)(2,1)}) fusion(f32[768,3072]{1,0:T(8,128)} %get-tuple-element.152, f32[768,3072]{1,0:T(8,128)} %get-tuple-element.182, f32[3072]{0:T(1024)S(1)} %copy-done.26, bf16[768,768]{0,1:T(8,128)(2,1)S(1)} %get-tuple-element.146, bf16[3072,768]{1,0:T(8,128)(2,1)S(1)} %copy-done.29), kind=kOutput, calls=%fused_computation.2 | convolution fusion | flops 3663983616 | bytes 29515776 | tf_op jit(solution)/shard_map/rd,fd->rf/dot_general | solution.py:317
  283.4 7.9 multiply_reduce_fusion
  301.7 19.0 %all_to_all.38 = bf16[768,4,192]{0,2,1:T(8,128)(2,1)} all-to-all(bf16[768,4,192]{0,2,1:T(8,128)(2,1)S(1)} %bitcast.147), channel_id=1, replica_groups=mesh['item'=8,'seq'=4] {'seq'}, dimensions={1} | all-to-all | bytes 2359296 | tf_op jit(solution)/shard_map/all_to_all | solution.py:330
  323.2 77.8 %attn_bwd.1 = bf16[3072,640]{1,0:T(8,128)(2,1)} custom-call(s32[1440]{0:T(1024)} %min.15.idx_ref, s32[5]{0:T(128)} %pad_add_fusion.2.gl_ref, bf16[3072,640]{1,0:T(8,128)(2,1)} %fusion.9.qkv_ref, bf16[3072,192]{1,0:T(8,128)(2,1)} %bitcast.143, f32[3072,128]{1,0:T(8,128)} %get-tuple-element.21.lse_ref, f32[144,640]{1,0:T(8,128)} %reshape.286.bias_ref), custom_call_target="tpu_custom_call" | custom-call | tf_op jit(solution)/shard_map/attn_bwd/pallas_call | solution.py:191
  401.0 7.8 fusion.22
  411.1 8.7 %convolution_convert_fusion.1 = bf16[3072,768]{1,0:T(8,128)(2,1)} fusion(bf16[768,3072]{1,0:T(8,128)(2,1)} %get-tuple-element.151, bf16[768,768]{0,1:T(8,128)(2,1)} %copy-done.11), kind=kOutput, calls=%fused_computation.21 | convolution fusion | flops 3626237952 | bytes 10616832 | tf_op jit(solution)/shard_map/rf,rd->fd/dot_general | solution.py:316
  420.5 9.2 %convolution_convert_fusion.2 = bf16[768,3072]{1,0:T(8,128)(2,1)} fusion(bf16[768,3072]{1,0:T(8,128)(2,1)} %get-tuple-element.144, f32[768,768]{0,1:T(8,128)} %copy-done, f32[768]{0:T(1024)} %get-tuple-element.121, f32[768]{0:T(1024)S(1)} %get-tuple-element.122, f32[768]{0:T(1024)S(1)} %copy-done.25, f32[768]{0:T(1024)S(1)} %broadcast_multiply_fusion.2), kind=kOutput, calls=%fused_computation.22 | convolution fusion | flops 3629187072 | bytes 11808768 | tf_op jit(solution)/shard_map/rd,rf->df/dot_general | solution.py:320
  430.1 8.5 %convolution_convert_fusion = bf16[3072,768]{0,1:T(8,128)(2,1)} fusion(bf16[3072,640]{1,0:T(8,128)(2,1)} %attn_bwd.1, bf16[768,640]{1,0:T(8,128)(2,1)} %copy-done.16), kind=kOutput, calls=%fused_computation.20 | convolution fusion | flops 3022258176 | bytes 9633792 | tf_op jit(solution)/shard_map/re,de->rd/dot_general | solution.py:333
  447.2 41.1 %psum.39 = f32[12,768]{1,0:T(8,128)} all-reduce(f32[12,768]{1,0:T(8,128)S(1)} %concatenate.37), channel_id=1, replica_groups=mesh['item'=8,'seq'=4] {'item','seq'}, use_global_device_ids=true, to_apply=%region_31.32 | all-reduce | flops 9216 | bytes 73728 | tf_op jit(solution)/shard_map/psum | solution.py:356
  490.4 11.7 %all_gather.23 = f32[96,3,4,192]{3,0,1,2:T(8,128)S(1)} all-gather(f32[96,3,1,192]{3,0,1,2:T(8,128)} %copy.109), channel_id=1, replica_groups=mesh['item'=8,'seq'=4] {'seq'}, dimensions={2}, use_global_device_ids=true | all-gather | bytes 1105920 | tf_op jit(solution)/shard_map/all_gather | solution.py:362
  503.0 70.3 %reduce-scatter.14.cloned.1.call-done = bf16[384,768]{1,0:T(8,128)(2,1)} async-done(((bf16[3072,768]{1,0:T(8,128)(2,1)}), bf16[384,768]{1,0:T(8,128)(2,1)}) %reduce-scatter.14.cloned.1.call-update) | async-done | bytes 589840 | tf_op jit(solution)/shard_map/reduce_scatter | solution.py:357
  573.2 99.1 %reduce-scatter.12.cloned.1.call-done = bf16[96,3072]{1,0:T(8,128)(2,1)} async-done(((bf16[768,3072]{1,0:T(8,128)(2,1)}), bf16[96,3072]{1,0:T(8,128)(2,1)}) %reduce-scatter.12.cloned.1.call-update) | async-done | bytes 589840 | tf_op jit(solution)/shard_map/reduce_scatter | solution.py:358
  672.3 75.1 %all-reduce.2 = (f32[96,768]{1,0:T(8,128)}, f32[96,3072]{1,0:T(8,128)}, f32[384,768]{1,0:T(8,128)}) all-reduce(bf16[96,768]{1,0:T(8,128)(2,1)} %reduce-scatter.10.cloned.1.call-done, bf16[96,3072]{1,0:T(8,128)(2,1)} %reduce-scatter.12.cloned.1.call-done, ...), channel_id=1, replica_groups=mesh['item'=8,'seq'=4] {'seq'}, use_global_device_ids=true, to_apply=%region_14.15 | all-reduce | flops 663552 | bytes 3981312 | tf_op jit(solution)/shard_map/psum | solution.py:363
  757.4 21.1 %psum.38 = f32[]{:T(128)} all-reduce(f32[]{:T(128)S(6)} %add.257), channel_id=1, replica_groups=mesh['item'=8,'seq'=4] {'item'}, use_global_device_ids=true, to_apply=%region_22.23 | all-reduce | flops 1 | bytes 8 | tf_op jit(solution)/shard_map/psum | solution.py:372
  786.5 4.1 multiply_subtract_fusion
  (205 shorter events, 77.4 us)
Async XLA Ops:
  7.2 44.9 %all-gather.12.cloned.1.call-start = ((), (), s32[]{:S(2)}) async-start(), calls=%async_computation.14 | async-start | bytes 5898240 | tf_op jit(solution)/shard_map/all_gather | solution.py:295
  7.9 137.7 %all-gather.6.cloned.1.call-start = ((), (), s32[]{:S(2)}) async-start(), calls=%async_computation.7 | async-start | bytes 1327104 | tf_op jit(solution)/shard_map/all_gather | solution.py:285
  9.7 166.0 %all-gather.8.cloned.1.call-start = ((), (), s32[]{:S(2)}) async-start(), calls=%async_computation.8 | async-start | bytes 5308416 | tf_op jit(solution)/shard_map/all_gather | solution.py:286
  10.7 245.7 %all-gather.10.cloned.1.call-start = ((), (), s32[]{:S(2)}) async-start(), calls=%async_computation.9 | async-start | bytes 5308416 | tf_op jit(solution)/shard_map/all_gather | solution.py:287
  11.6 36.8 %copy-start.30 = (s32[1,4]{1,0:T(1,128)S(1)}, s32[1,4]{1,0:T(1,128)}, u32[]{:S(2)}) copy-start(s32[1,4]{1,0:T(1,128)} %param.23) | copy-start | bytes 52
  11.7 36.9 %copy-start.27 = (s32[1,3,48,3]{2,0,3,1:T(1,128)S(1)}, s32[1,3,48,3]{2,0,3,1:T(1,128)}, u32[]{:S(2)}) copy-start(s32[1,3,48,3]{2,0,3,1:T(1,128)} %param.24) | copy-start | bytes 5188
  47.8 12.4 %copy-start.16 = (bf16[768,640]{1,0:T(8,128)(2,1)}, bf16[768,640]{1,0:T(8,128)(2,1)S(1)}, u32[]{:S(2)}) copy-start(bf16[768,640]{1,0:T(8,128)(2,1)S(1)} %all_gather.18) | copy-start | bytes 2949124
  135.6 7.3 copy-start.1
  138.2 6.1 slice-start
  138.2 6.8 copy-start.13
  138.2 20.3 %all-to-all-start = ((bf16[4,768,192]{1,2,0:T(8,128)(2,1)}), bf16[4,768,192]{1,2,0:T(8,128)(2,1)}, u32[]{:S(2)}, u32[]{:S(2)}) async-start(bf16[4,768,192]{1,2,0:T(8,128)(2,1)} %copy.104), calls=%async_computation | async-start | bytes 2359296 | tf_op jit(solution)/shard_map/all_to_all | solution.py:301
  142.6 15.9 %copy-start.28 = (f32[768]{0:T(1024)S(1)}, f32[768]{0:T(1024)}, u32[]{:S(2)}) copy-start(f32[768]{0:T(1024)} %get-tuple-element.123) | copy-start | bytes 9220
  142.6 345.7 %reduce-scatter.10.cloned.1.call-start = ((), (), s32[]{:S(2)}) async-start(), calls=%async_computation.11 | async-start | bytes 1327104 | tf_op jit(solution)/shard_map/reduce_scatter | solution.py:359
  161.7 121.6 %copy-start = (f32[768,768]{0,1:T(8,128)}, f32[768,768]{0,1:T(8,128)S(1)}, u32[]{:S(2)}) copy-start(f32[768,768]{0,1:T(8,128)S(1)} %get-tuple-element.181) | copy-start | bytes 7077892
  265.1 4.6 copy-start.29
  267.0 16.3 %slice-start.1 = ((s8[4718592]{0:T(1024)(128)(4,1)}), s8[4194304]{0:T(1024)(128)(4,1)S(1)}, s32[]{:S(2)}) async-start(s8[4718592]{0:T(1024)(128)(4,1)} %bitcast.151), calls=%async_computation.17 | async-start | bytes 8388608
  269.8 13.6 %copy-start.11 = (bf16[768,768]{0,1:T(8,128)(2,1)}, bf16[768,768]{0,1:T(8,128)(2,1)S(1)}, u32[]{:S(2)}) copy-start(bf16[768,768]{0,1:T(8,128)(2,1)S(1)} %get-tuple-element.146) | copy-start | bytes 3538948
  269.8 13.6 %copy-start.24 = (f32[768]{0:T(1024)S(1)}, f32[768]{0:T(1024)}, u32[]{:S(2)}) copy-start(f32[768]{0:T(1024)} %fusion.37) | copy-start | bytes 9220
  269.8 13.6 %slice-start.2 = ((s8[4718592]{0:T(1024)(128)(4,1)}), s8[524288]{0:T(1024)(128)(4,1)S(1)}, s32[]{:S(2)}) async-start(s8[4718592]{0:T(1024)(128)(4,1)} %bitcast.151), calls=%async_computation.18 | async-start | bytes 1048576
  299.0 189.3 %reduce-scatter.16.cloned.1.call-start = ((), (), s32[]{:S(2)}) async-start(), calls=%async_computation.15 | async-start | bytes 1105920
  411.0 162.2 %reduce-scatter.14.cloned.1.call-start = ((), (), s32[]{:S(2)}) async-start(), calls=%async_computation.13 | async-start | bytes 5308416 | tf_op jit(solution)/shard_map/reduce_scatter | solution.py:357
  419.8 252.5 %reduce-scatter.12.cloned.1.call-start = ((), (), s32[]{:S(2)}) async-start(), calls=%async_computation.12 | async-start | bytes 5308416 | tf_op jit(solution)/shard_map/reduce_scatter | solution.py:358
  429.8 366.0 %reduce-scatter.8.cloned.1.call-start = ((), (), s32[]{:S(2)}) async-start(), calls=%async_computation.10 | async-start | bytes 5898240 | tf_op jit(solution)/shard_map/reduce_scatter | solution.py:334
  786.4 4.2 copy-start.5
  (20 other events, 54.7 us)
Sparse Core Ops, SparseCore 0:
  9.6 40.1 all-gather.11
  52.6 41.3 all-gather.5
  96.8 78.8 all-gather.7
  178.3 78.0 all-gather.9
  299.1 62.4 reduce-scatter.9
  411.1 63.1 reduce-scatter.15
  478.4 94.7 reduce-scatter.13
  577.3 94.9 reduce-scatter.11
  675.0 69.2 reduce-scatter.7

commit v2 on v1

v2 whole, which is shorter than its diff:
```python
import functools

import jax
import jax.numpy as jnp
from jax import lax
from jax.experimental import pallas as pl
from jax.experimental.pallas import tpu as pltpu
from jax.sharding import PartitionSpec as P

ADAM_STEP = 10
norm_epsilon = 1e-06
beta_first = 0.9
beta_second = 0.999
adam_epsilon = 1e-08
learn_rate = 0.1
small_rate = 0.5
weight_decay = 0.01
clip_level = 1.0


HD = 64
BL = 64
NEG = -1e30
bf16 = jnp.bfloat16
f32 = jnp.float32
NT = (((1,), (1,)), ((), ()))
TN = (((0,), (0,)), ((), ()))


def slots(count, positions, table, place):
    heads, nblocks, picks = table.shape
    chunk = nblocks // 4
    globals_n = positions.shape[0]
    here = jnp.arange(nblocks, dtype=jnp.int32)

    def turned(b):
        return ((b // chunk) ^ place) * chunk + b % chunk

    block = turned(here)
    rows = table.reshape(heads, 2, 2, chunk, picks)
    rows = jnp.where(place % 2 == 1, rows[:, :, ::-1], rows)
    rows = jnp.where(place // 2 == 1, rows[:, ::-1], rows).reshape(heads, nblocks, picks)
    window = jnp.stack([block - 1, block, block + 1], -1)
    active = jnp.arange(globals_n, dtype=jnp.int32) < count
    parts = jnp.concatenate(
        [
            jnp.broadcast_to(window[None], (heads, nblocks, 3)),
            jnp.broadcast_to(jnp.where(active, positions, -1)[None, None], (heads, nblocks, globals_n)),
            rows,
        ],
        -1,
    )
    count_slots = 3 + globals_n + picks
    valid = (parts >= 0) & (parts < nblocks)
    same = parts[..., :, None] == parts[..., None, :]
    earlier = jnp.arange(count_slots)[:, None] > jnp.arange(count_slots)[None, :]
    repeated = jnp.any(same & earlier, -1)
    is_global = jnp.any((positions[None, :] == block[:, None]) & active[None], -1)
    valid = valid & ~repeated & ~is_global[None, :, None]
    idx = turned(jnp.clip(parts, 0, nblocks - 1))
    bias = jnp.where(valid, 0.0, NEG).astype(f32)
    bias = jnp.broadcast_to(bias[..., None], (heads, nblocks, count_slots, BL))
    glob = jnp.concatenate([count[None], turned(positions)])
    return idx.reshape(-1), bias.reshape(heads * nblocks, count_slots * BL), glob


def low_lanes(rows):
    return lax.broadcasted_iota(jnp.int32, (rows, 2 * HD), 1) < HD


def pick(block, keep_low):
    low = low_lanes(block.shape[0])
    return jnp.where(low if keep_low else ~low, block, jnp.zeros_like(block))


def fwd_kernel(dims, idx_ref, gl_ref, qkv_ref, bias_ref, *rest):
    heads, nblocks, slots_n, first, parts, chunk, wide = dims
    out_refs, lse_ref, sbuf = rest[:parts], rest[parts], rest[parts + 1]
    n = nblocks * BL
    lane = lax.broadcasted_iota(jnp.int32, (BL, 128), 1)

    def finish(out_ref, at, row, outs, lses):
        low = low_lanes(BL)
        for p in range((heads + 1) // 2):
            if 2 * p + 1 < heads:
                both = jnp.where(low, outs[2 * p], outs[2 * p + 1])
                out_ref[pl.ds(at, BL), p * 128 : (p + 1) * 128] = both.astype(bf16)
            else:
                out_ref[pl.ds(at, BL), p * 128 : p * 128 + HD] = outs[2 * p][:, :HD].astype(bf16)
        total = jnp.zeros((BL, 128), f32)
        for h in range(heads):
            total = jnp.where(lane == h, lses[h], total)
        lse_ref[pl.ds(row, BL), :] = total

    def queries(r, h):
        return pick(qkv_ref[pl.ds(r, BL), (heads + h // 2) * 128 : (heads + h // 2 + 1) * 128], h % 2 == 1)

    for part in range(parts):

        def body(b, _):
            a = first + part * chunk + b
            r = pl.multiple_of(a * BL, BL)
            outs, lses = [], []
            for h in range(heads):
                base = (h * nblocks + a) * slots_n
                kv = jnp.concatenate(
                    [
                        qkv_ref[pl.ds(pl.multiple_of(idx_ref[base + j] * BL, BL), BL), h * 128 : (h + 1) * 128]
                        for j in range(slots_n)
                    ],
                    0,
                )
                s = lax.dot_general(queries(r, h), kv, NT, preferred_element_type=f32)
                s = s + bias_ref[pl.ds(h * nblocks + a, 1), :]
                m = jnp.max(s, -1, keepdims=True)
                e = jnp.exp(s - m)
                l = jnp.sum(e, -1, keepdims=True)
                p = (e * (1.0 / l)).astype(bf16)
                outs.append(jnp.dot(p, kv, preferred_element_type=f32))
                lses.append(m + jnp.log(l))
            at = pl.multiple_of(b * BL, BL)
            finish(out_refs[part], at, pl.multiple_of(part * chunk * BL + at, BL), outs, lses)
            return 0

        lax.fori_loop(0, chunk, body, 0)

    def whole_row(g, _):
        a = gl_ref[1 + g]
        local = a - first

        @pl.when((local >= 0) & (local < parts * chunk))
        def _():
            r = pl.multiple_of(a * BL, BL)
            outs, lses = [], []
            for h in range(heads):
                q = queries(r, h)
                m = None
                for c in range(n // wide):
                    cs = slice(c * wide, (c + 1) * wide)
                    s = lax.dot_general(q, qkv_ref[cs, h * 128 : (h + 1) * 128], NT, preferred_element_type=f32)
                    sbuf[h, :, cs] = s
                    mc = jnp.max(s, -1, keepdims=True)
                    m = mc if m is None else jnp.maximum(m, mc)
                l = 0.0
                for c in range(n // wide):
                    cs = slice(c * wide, (c + 1) * wide)
                    e = jnp.exp(sbuf[h, :, cs] - m)
                    sbuf[h, :, cs] = e
                    l = l + jnp.sum(e, -1, keepdims=True)
                inv = 1.0 / l
                o = 0.0
                for c in range(n // wide):
                    cs = slice(c * wide, (c + 1) * wide)
                    p = (sbuf[h, :, cs] * inv).astype(bf16)
                    o = o + jnp.dot(p, qkv_ref[cs, h * 128 : (h + 1) * 128], preferred_element_type=f32)
                outs.append(o)
                lses.append(m + jnp.log(l))
            row = pl.multiple_of(local * BL, BL)
            for part in range(parts):

                @pl.when(local // chunk == part)
                def _():
                    finish(out_refs[part], pl.multiple_of(row - part * chunk * BL, BL), row, outs, lses)

        return 0

    lax.fori_loop(0, gl_ref[0], whole_row, 0)


def attn_fwd(idx, gl, qkv, bias, heads, first_part, parts):
    n = qkv.shape[0]
    nblocks = n // BL
    chunk = nblocks // 4
    slots_n = bias.shape[1] // BL
    vmem = pl.BlockSpec(memory_space=pltpu.VMEM)
    smem = pl.BlockSpec(memory_space=pltpu.SMEM)
    dims = (heads, nblocks, slots_n, first_part * chunk, parts, chunk, 512)
    return pl.pallas_call(
        functools.partial(fwd_kernel, dims),
        out_shape=tuple([jax.ShapeDtypeStruct((n // 4, heads * HD), bf16)] * parts)
        + (jax.ShapeDtypeStruct((parts * n // 4, 128), f32),),
        in_specs=[smem, smem, vmem, vmem],
        out_specs=tuple([vmem] * (parts + 1)),
        scratch_shapes=[pltpu.VMEM((heads, BL, n), f32)],
        compiler_params=pltpu.CompilerParams(vmem_limit_bytes=56 << 20),
        cost_estimate=pl.CostEstimate(flops=10 * parts * 10**9, bytes_accessed=10**7, transcendentals=0),
        name="attn_fwd",
    )(idx, gl, qkv, bias)


def bwd_kernel(dims, idx_ref, gl_ref, qkv_ref, bias_ref, *rest):
    heads, nblocks, slots_n, first, parts, chunk, wide, begin, end = dims
    g_refs, rest = rest[:parts], rest[parts:]
    lse_ref, rest = rest[0], rest[1:]
    if not begin:
        acc_in, dq_in, rest = rest[0], rest[1], rest[2:]
    if end:
        out_ref, acc, pbuf, dbuf = rest
    else:
        acc, dq_ref, pbuf, dbuf = rest
    n = nblocks * BL
    pairs = (heads + 1) // 2
    kvw = heads * 128

    def start(i, _):
        rr = pl.ds(pl.multiple_of(i * 256, 256), 256)
        if begin:
            acc[rr, :] = jnp.zeros((256, kvw), f32)
        else:
            acc[rr, :] = acc_in[rr, :]
        return 0

    lax.fori_loop(0, n // 256, start, 0)
    if end and not begin:
        out_ref[0 : first * BL, kvw:] = dq_in[...]

    def grads(g_ref, at, h):
        w = min(128, heads * HD - (h // 2) * 128)
        g = g_ref[pl.ds(at, BL), (h // 2) * 128 : (h // 2) * 128 + w]
        if w < 128:
            return jnp.concatenate([g, jnp.zeros((BL, 128 - w), bf16)], 1)
        return pick(g, h % 2 == 0)

    def queries(r, h):
        return pick(qkv_ref[pl.ds(r, BL), (heads + h // 2) * 128 : (heads + h // 2 + 1) * 128], h % 2 == 1)

    def finish(r, dqs):
        low = low_lanes(BL)
        for p in range(pairs):
            high = dqs[2 * p]
            odd = dqs[2 * p + 1] if 2 * p + 1 < heads else jnp.zeros_like(high)
            both = jnp.where(low, odd, high).astype(bf16)
            if end:
                out_ref[pl.ds(r, BL), kvw + p * 128 : kvw + (p + 1) * 128] = both
            else:
                dq_ref[pl.ds(pl.multiple_of(r - first * BL, BL), BL), p * 128 : (p + 1) * 128] = both

    for part in range(parts):

        def body(b, _):
            a = first + part * chunk + b
            r = pl.multiple_of(a * BL, BL)
            at = pl.multiple_of(b * BL, BL)
            row = pl.multiple_of(part * chunk * BL + at, BL)
            dqs = []
            for h in range(heads):
                hs = slice(h * 128, (h + 1) * 128)
                x = jnp.concatenate([queries(r, h), grads(g_refs[part], at, h)], 0)
                base = (h * nblocks + a) * slots_n
                rows = [pl.multiple_of(idx_ref[base + j] * BL, BL) for j in range(slots_n)]
                kv = jnp.concatenate([qkv_ref[pl.ds(rows[j], BL), hs] for j in range(slots_n)], 0)
                sd = lax.dot_general(x, kv, NT, preferred_element_type=f32)
                p = jnp.exp(sd[:BL] + bias_ref[pl.ds(h * nblocks + a, 1), :] - lse_ref[pl.ds(row, BL), h : h + 1])
                dp = sd[BL:]
                ds = p * (dp - jnp.sum(dp * p, -1, keepdims=True))
                w = jnp.concatenate([ds.astype(bf16), p.astype(bf16)], 0)
                dqs.append(jnp.dot(w[:BL], kv, preferred_element_type=f32))
                dkv = lax.dot_general(w, x, TN, preferred_element_type=f32)
                for j in range(slots_n):
                    acc[pl.ds(rows[j], BL), hs] += dkv[j * BL : (j + 1) * BL]
            finish(r, dqs)
            return 0

        lax.fori_loop(0, chunk, body, 0)

    def whole_row(g, _):
        a = gl_ref[1 + g]
        local = a - first
        for part in range(parts):

            @pl.when((local >= part * chunk) & (local < (part + 1) * chunk))
            def _():
                r = pl.multiple_of(a * BL, BL)
                row = pl.multiple_of(local * BL, BL)
                at = pl.multiple_of((local - part * chunk) * BL, BL)
                dqs = []
                for h in range(heads):
                    hs = slice(h * 128, (h + 1) * 128)
                    x = jnp.concatenate([queries(r, h), grads(g_refs[part], at, h)], 0)
                    lse = lse_ref[pl.ds(row, BL), h : h + 1]
                    inner = 0.0
                    for c in range(n // wide):
                        cs = slice(c * wide, (c + 1) * wide)
                        sd = lax.dot_general(x, qkv_ref[cs, hs], NT, preferred_element_type=f32)
                        p = jnp.exp(sd[:BL] - lse)
                        dp = sd[BL:]
                        pbuf[h, :, cs] = p
                        dbuf[h, :, cs] = dp
                        inner = inner + jnp.sum(dp * p, -1, keepdims=True)
                    dq = 0.0
                    for c in range(n // wide):
                        cs = slice(c * wide, (c + 1) * wide)
                        p = pbuf[h, :, cs]
                        ds = (p * (dbuf[h, :, cs] - inner)).astype(bf16)
                        w = jnp.concatenate([ds, p.astype(bf16)], 0)
                        dq = dq + jnp.dot(ds, qkv_ref[cs, hs], preferred_element_type=f32)
                        acc[cs, hs] += lax.dot_general(w, x, TN, preferred_element_type=f32)
                    dqs.append(dq)
                finish(r, dqs)

        return 0

    lax.fori_loop(0, gl_ref[0], whole_row, 0)
    if end:

        def flush(i, _):
            rr = pl.ds(pl.multiple_of(i * 256, 256), 256)
            out_ref[rr, :kvw] = acc[rr, :].astype(bf16)
            return 0

        lax.fori_loop(0, n // 256, flush, 0)


def attn_bwd(idx, gl, qkv, bias, grads, lse, heads, first_part, carried, end):
    n = qkv.shape[0]
    nblocks = n // BL
    chunk = nblocks // 4
    slots_n = bias.shape[1] // BL
    parts = len(grads)
    vmem = pl.BlockSpec(memory_space=pltpu.VMEM)
    smem = pl.BlockSpec(memory_space=pltpu.SMEM)
    dims = (heads, nblocks, slots_n, first_part * chunk, parts, chunk, 512, not carried, end)
    pairs = (heads + 1) // 2
    scratch = [pltpu.VMEM((heads, BL, n), f32)] * 2
    if end:
        out_shape = jax.ShapeDtypeStruct((n, (heads + pairs) * 128), bf16)
        out_specs = vmem
        scratch = [pltpu.VMEM((n, heads * 128), f32)] + scratch
    else:
        out_shape = (
            jax.ShapeDtypeStruct((n, heads * 128), f32),
            jax.ShapeDtypeStruct((parts * n // 4, pairs * 128), bf16),
        )
        out_specs = (vmem, vmem)
    return pl.pallas_call(
        functools.partial(bwd_kernel, dims),
        out_shape=out_shape,
        in_specs=[smem, smem] + [vmem] * (3 + parts + len(carried)),
        out_specs=out_specs,
        scratch_shapes=scratch,
        compiler_params=pltpu.CompilerParams(vmem_limit_bytes=60 << 20),
        cost_estimate=pl.CostEstimate(flops=11 * parts * 10**9, bytes_accessed=10**7, transcendentals=0),
        name="attn_bwd",
    )(idx, gl, qkv, bias, *grads, lse, *carried)


MESH_ID = pl.DeviceIdType.MESH


def flip(index, number):
    total = 0
    for bit in (1, 2, 4):
        digit = (index // bit) % 2
        total = total + bit * ((1 - digit) if number & bit else digit)
    return total


def greet(item, place, items):
    barrier = pltpu.get_barrier_semaphore()
    for t in range(1, 4):
        pl.semaphore_signal(barrier, inc=1, device_id=(item, flip(place, t)), device_id_type=MESH_ID)
    for k in range(1, items):
        pl.semaphore_signal(barrier, inc=1, device_id=(flip(item, k), place), device_id_type=MESH_ID)
    pl.semaphore_wait(barrier, 3 + items - 1)


def tail_kernel(
    items, query_columns, x0, x1, x2, x3, gq_ref, slab_ref, first_ref, small_ref, shard_ref,
    din_ref, group_ref, total_ref, squares_ref,
    near_out, near_in, far_out, far_in, grad_v, part_out, part_in, small_in, small_mid, small_items, sq_out, sq_in, sq_mid, sq_items,
    near_send, near_recv, far_send, far_recv, part_send, part_recv, sg_send, sg_recv, si_send, si_recv,
    gr_send, gr_recv, qg_send, qg_recv, qi_send, qi_recv,
):
    xs = (x0, x1, x2, x3)
    item, place = lax.axis_index("item"), lax.axis_index("seq")
    tokens, width = x0.shape
    rows = width // items
    tile = 256
    chunks = tokens // tile
    columns = gq_ref.shape[1]
    small_rows = small_ref.shape[0]
    greet(item, place, items)

    def to_group(src, dst, send, recv, t):
        return pltpu.make_async_remote_copy(
            src_ref=src, dst_ref=dst, send_sem=send, recv_sem=recv,
            device_id=(item, flip(place, t)), device_id_type=MESH_ID,
        )

    def to_item(src, dst, send, recv, k):
        return pltpu.make_async_remote_copy(
            src_ref=src, dst_ref=dst, send_sem=send, recv_sem=recv,
            device_id=(flip(item, k), place), device_id_type=MESH_ID,
        )

    small_copies = [to_group(small_ref, small_in.at[t], sg_send.at[t], sg_recv.at[t], t) for t in range(1, 4)]
    for copy in small_copies:
        copy.start()

    def token_part(t, c):
        return lax.dot_general(
            gq_ref[t * tokens + c * tile : t * tokens + (c + 1) * tile, :], slab_ref[...], NT, preferred_element_type=f32
        )

    near_copies = {}
    far_copies = []

    def send_near(t):
        for c in range(chunks):
            cs = pl.ds(c * tile, tile)
            near_out[t // 2, c * tile : (c + 1) * tile, :] = token_part(t, c).astype(bf16)
            copy = to_group(
                near_out.at[t // 2, cs], near_in.at[t // 2, cs], near_send.at[t // 2, c], near_recv.at[t // 2, c], 1
            )
            copy.start()
            near_copies[(t // 2, c)] = copy

    send_near(3)
    for c in range(chunks):
        cs = slice(c * tile, (c + 1) * tile)
        part = token_part(2, c)
        near_copies[(1, c)].wait_recv()
        far_out[cs, :] = (part.astype(bf16).astype(f32) + near_in[1, cs, :].astype(f32)).astype(bf16)
        copy = to_group(far_out.at[pl.ds(c * tile, tile)], far_in.at[pl.ds(c * tile, tile)], far_send.at[c], far_recv.at[c], 2)
        copy.start()
        far_copies.append(copy)

    def slab_rows(r, _):
        at = pl.multiple_of(r * tile, tile)
        part = 0.0
        for t in range(4):
            part = part + lax.dot_general(
                xs[t][:, pl.ds(at, tile)], gq_ref[t * tokens : (t + 1) * tokens, :], TN, preferred_element_type=f32
            )
        grad_v[pl.ds(at, tile), :] = part
        return 0

    lax.fori_loop(0, width // tile, slab_rows, 0)

    def sums(r, line):
        at = pl.multiple_of(r * tile, tile)
        return line + jnp.sum(gq_ref[pl.ds(at, tile), :].astype(f32), 0, keepdims=True)

    line = lax.fori_loop(0, 4 * chunks, sums, jnp.zeros((1, columns), f32))
    high = line.astype(bf16)
    rest = (line - high.astype(f32)).astype(bf16)
    which = lax.broadcasted_iota(jnp.int32, (16, columns), 0)
    lines = jnp.where(which == 0, high.astype(f32), jnp.where(which == 1, rest.astype(f32), 0.0)).astype(bf16)
    part_copies = []
    for k in list(range(items - 1, 0, -1)) + [0]:
        at = pl.multiple_of(flip(item, k) * rows, 8)
        part_out[k, 0:rows, :] = grad_v[pl.ds(at, rows), :].astype(bf16)
        part_out[k, rows : rows + 16, :] = lines
        if k:
            copy = to_item(part_out.at[k], part_in.at[k], part_send.at[k], part_recv.at[k], k)
            copy.start()
            part_copies.append(copy)

    for copy in small_copies:
        copy.wait()
    small_mid[...] = small_ref[...] + small_in[1] + small_in[2] + small_in[3]
    item_copies = [to_item(small_mid, small_items.at[k], si_send.at[k], si_recv.at[k], k) for k in range(1, items)]
    for copy in item_copies:
        copy.start()

    send_near(1)
    for c in range(chunks):
        cs = slice(c * tile, (c + 1) * tile)
        din_ref[cs, :] = first_ref[cs, :] + token_part(0, c).astype(bf16).astype(f32)

    def square_sum(values):
        return jnp.sum(jnp.sum(values * values, 0, keepdims=True), -1, keepdims=True)

    squares = square_sum(shard_ref[...])
    for copy in part_copies:
        copy.wait()
    own = part_out[0].astype(f32)
    for k in range(1, items):
        own = own + part_in[k].astype(f32)
    group_ref[0] = own
    group_copies = [to_group(group_ref.at[0], group_ref.at[t], gr_send.at[t], gr_recv.at[t], t) for t in (2, 1)]
    for copy in group_copies:
        copy.start()
    column = lax.broadcasted_iota(jnp.int32, (1, columns), 1)
    squares = squares + square_sum(own[0:rows] * jnp.where(column < query_columns, 1.0, HD**-0.5))
    sq_out[...] = jnp.broadcast_to(squares, (8, 128))
    sq_copies = [to_group(sq_out, sq_in.at[t], qg_send.at[t], qg_recv.at[t], t) for t in range(1, 4)]
    for copy in sq_copies:
        copy.start()
    for copy in sq_copies:
        copy.wait()
    sq_mid[...] = sq_out[...] + sq_in[1] + sq_in[2] + sq_in[3]
    sq_item_copies = [to_item(sq_mid, sq_items.at[k], qi_send.at[k], qi_recv.at[k], k) for k in range(1, items)]
    for copy in sq_item_copies:
        copy.start()

    group_copies[0].wait()
    cross = to_group(group_ref.at[2], group_ref.at[3], gr_send.at[3], gr_recv.at[3], 1)
    cross.start()
    for copy in item_copies:
        copy.wait()
    total = small_mid[...]
    for k in range(1, items):
        total = total + small_items[k]
    total_ref[...] = total
    for c in range(chunks):
        cs = slice(c * tile, (c + 1) * tile)
        near_copies[(1, c)].wait_send()
        near_copies[(0, c)].wait()
        far_copies[c].wait()
        din_ref[cs, :] = din_ref[cs, :] + near_in[0, cs, :].astype(f32) + far_in[cs, :].astype(f32)
    for copy in sq_item_copies:
        copy.wait()
    answer = sq_mid[...]
    for k in range(1, items):
        answer = answer + sq_items[k]
    squares_ref[...] = answer
    group_copies[1].wait()
    cross.wait()


def tail(xs, gq, slab, first, small, shard, items, query_columns):
    tokens, width = xs[0].shape
    columns = gq.shape[1]
    rows = width // items
    vmem = pl.BlockSpec(memory_space=pltpu.VMEM)
    dma = pltpu.SemaphoreType.DMA
    chunks = tokens // 256
    return pl.pallas_call(
        functools.partial(tail_kernel, items, query_columns),
        out_shape=(
            jax.ShapeDtypeStruct((tokens, width), f32),
            jax.ShapeDtypeStruct((4, rows + 16, columns), f32),
            jax.ShapeDtypeStruct(small.shape, f32),
            jax.ShapeDtypeStruct((8, 128), f32),
        ),
        in_specs=[vmem] * 9,
        out_specs=(vmem,) * 4,
        scratch_shapes=[
            pltpu.VMEM((2, tokens, width), bf16),
            pltpu.VMEM((2, tokens, width), bf16),
            pltpu.VMEM((tokens, width), bf16),
            pltpu.VMEM((tokens, width), bf16),
            pltpu.VMEM((width, columns), f32),
            pltpu.VMEM((items, rows + 16, columns), bf16),
            pltpu.VMEM((items, rows + 16, columns), bf16),
            pltpu.VMEM((4,) + small.shape, f32),
            pltpu.VMEM(small.shape, f32),
            pltpu.VMEM((items,) + small.shape, f32),
            pltpu.VMEM((8, 128), f32),
            pltpu.VMEM((4, 8, 128), f32),
            pltpu.VMEM((8, 128), f32),
            pltpu.VMEM((items, 8, 128), f32),
            dma((2, chunks)), dma((2, chunks)), dma((chunks,)), dma((chunks,)),
            dma((items,)), dma((items,)), dma((4,)), dma((4,)), dma((items,)), dma((items,)),
            dma((4,)), dma((4,)), dma((4,)), dma((4,)), dma((items,)), dma((items,)),
        ],
        compiler_params=pltpu.CompilerParams(vmem_limit_bytes=60 << 20, collective_id=3, has_side_effects=True),
        cost_estimate=pl.CostEstimate(flops=60 * 10**9, bytes_accessed=10**7, transcendentals=0),
        name="tail",
    )(*xs, gq, slab, first, small, shard)
def project_kernel(item_of, tile, *refs):
    items = len(refs) - 7
    xs, pieces, bias_ref, out_ref, slab_ref = refs[:4], refs[4:-3], refs[-3], refs[-2], refs[-1]
    item = item_of()
    rows = pieces[0].shape[0]
    for k in range(items):
        at = pl.multiple_of((item ^ k) * rows, 16)
        slab_ref[pl.ds(at, rows), :] = pieces[k][...]
    tokens = xs[0].shape[0]
    for t in range(4):

        def body(r, _):
            at = pl.multiple_of(r * tile, tile)
            part = jnp.dot(xs[t][pl.ds(at, tile), :], slab_ref[...], preferred_element_type=f32)
            out_ref[pl.ds(pl.multiple_of(t * tokens + at, tile), tile), :] = (part + bias_ref[...]).astype(bf16)
            return 0

        lax.fori_loop(0, tokens // tile, body, 0)


def project(item_of, xs, pieces, bias):
    tokens, width = xs[0].shape
    rows, columns = pieces[0].shape
    vmem = pl.BlockSpec(memory_space=pltpu.VMEM)
    return pl.pallas_call(
        functools.partial(project_kernel, item_of, 256),
        out_shape=(
            jax.ShapeDtypeStruct((4 * tokens, columns), bf16),
            jax.ShapeDtypeStruct((rows * len(pieces), columns), bf16),
        ),
        in_specs=[vmem] * (5 + len(pieces)),
        out_specs=(vmem, vmem),
        compiler_params=pltpu.CompilerParams(vmem_limit_bytes=48 << 20),
        cost_estimate=pl.CostEstimate(flops=6 * 10**9, bytes_accessed=10**7, transcendentals=0),
        name="project",
    )(*xs, *pieces, bias)


def token_grad_kernel(tile, gq_ref, slab_ref, keep_ref, send_ref):
    tokens = keep_ref.shape[1]
    for t in (1, 3, 0, 2):
        out_ref = send_ref if t % 2 else keep_ref

        def body(r, _):
            at = pl.multiple_of(r * tile, tile)
            part = lax.dot_general(
                gq_ref[pl.ds(pl.multiple_of(t * tokens + at, tile), tile), :],
                slab_ref[...],
                NT,
                preferred_element_type=f32,
            )
            out_ref[t // 2, pl.ds(at, tile), :] = part.astype(bf16)
            return 0

        lax.fori_loop(0, tokens // tile, body, 0)


def token_grads(gq, slab):
    tokens, width = gq.shape[0] // 4, slab.shape[0]
    vmem = pl.BlockSpec(memory_space=pltpu.VMEM)
    half = jax.ShapeDtypeStruct((2, tokens, width), bf16)
    return pl.pallas_call(
        functools.partial(token_grad_kernel, 256),
        out_shape=(half, half),
        in_specs=[vmem] * 2,
        out_specs=(vmem, vmem),
        compiler_params=pltpu.CompilerParams(vmem_limit_bytes=48 << 20),
        cost_estimate=pl.CostEstimate(flops=6 * 10**9, bytes_accessed=10**7, transcendentals=0),
        name="token_grads",
    )(gq, slab)


def slab_grad_kernel(item_of, items, *refs):
    xs, gq_ref, sums_ref, part_refs, total = refs[:4], refs[4], refs[5], refs[6 : 6 + items], refs[6 + items]
    item = item_of()
    tokens, width = xs[0].shape
    rows = width // items
    tile = 256
    for t in range(4):

        def body(r, _):
            at = pl.multiple_of(r * tile, tile)
            part = lax.dot_general(
                xs[t][:, pl.ds(at, tile)], gq_ref[t * tokens : (t + 1) * tokens, :], TN, preferred_element_type=f32
            )
            if t == 0:
                total[pl.ds(at, tile), :] = part
            else:
                total[pl.ds(at, tile), :] += part
            return 0

        lax.fori_loop(0, width // tile, body, 0)
    for k in range(items):
        part_refs[k][...] = total[pl.ds(pl.multiple_of((item ^ k) * rows, 8), rows), :].astype(bf16)

    def sums(r, total_row):
        at = pl.multiple_of(r * tile, tile)
        return total_row + jnp.sum(gq_ref[pl.ds(at, tile), :].astype(f32), 0, keepdims=True)

    sums_ref[...] = lax.fori_loop(0, gq_ref.shape[0] // tile, sums, jnp.zeros((1, gq_ref.shape[1]), f32))


def slab_grads(item_of, xs, gq, items):
    tokens, width = xs[0].shape
    columns = gq.shape[1]
    vmem = pl.BlockSpec(memory_space=pltpu.VMEM)
    return pl.pallas_call(
        functools.partial(slab_grad_kernel, item_of, items),
        out_shape=(jax.ShapeDtypeStruct((1, columns), f32),)
        + tuple([jax.ShapeDtypeStruct((width // items, columns), bf16)] * items),
        in_specs=[vmem] * 5,
        out_specs=tuple([vmem] * (1 + items)),
        scratch_shapes=[pltpu.VMEM((width, columns), f32)],
        compiler_params=pltpu.CompilerParams(vmem_limit_bytes=48 << 20),
        cost_estimate=pl.CostEstimate(flops=6 * 10**9, bytes_accessed=10**7, transcendentals=0),
        name="slab_grads",
    )(*xs, gq)


def gelu_parts(u):
    half = 0.5 * (1.0 + lax.erf(u * 0.7071067811865476))
    return u * half, half + u * jnp.exp(-0.5 * u * u) * 0.3989422804014327


def middle_kernel(
    dims, where_am_i, own_ref, far_ref, near_ref, x_ref, mixed_ref, dout_ref, small_ref,
    out_ref, first_ref, gmix_ref, grads_ref, sgrad_ref,
    wo_v, wu_v, wd_v, xhat_v, hid_v, act_v, slope_v, ffn_v, gffn_v, gup_v, dhid_v, rstd_v, stage_d, stage_u, stage_o,
    wsem, gsem,
):
    items, rows, width, tile = dims
    item, place = where_am_i()
    third = rows // 3
    tokens = x_ref.shape[0]
    tiles = tokens // tile
    group_rows = width // 4
    sources = (own_ref, near_ref.at[0], far_ref, near_ref.at[1])

    def load(which):
        for t in range(4):
            q = place ^ t
            for k in range(items):
                j = item ^ k
                src = sources[t].at[k]
                if which == 0:
                    pltpu.make_async_copy(src.at[pl.ds(2 * rows, third)], wo_v.at[j, pl.ds(pl.multiple_of(q * third, 16), third)], wsem.at[0]).start()
                elif which == 1:
                    pltpu.make_async_copy(src.at[pl.ds(0, rows)], wu_v.at[q, pl.ds(pl.multiple_of(j * rows, 16), rows)], wsem.at[1]).start()
                else:
                    pltpu.make_async_copy(src.at[pl.ds(rows, rows)], wd_v.at[j // 2, pl.ds(pl.multiple_of((j % 2) * 4 * rows + q * rows, 16), rows)], wsem.at[2]).start()

    for which in range(3):
        load(which)

    def rowsl(r):
        return pl.ds(pl.multiple_of(r * tile, tile), tile)

    def wo_rows(q):
        return jnp.concatenate([wo_v[2 * q, 0:rows], wo_v[2 * q + 1, 0:rows]], 0)

    pltpu.make_async_copy(wo_v, wo_v, wsem.at[0]).wait()

    def norm_one(r, _):
        rs = rowsl(r)
        total = x_ref[rs, :].astype(f32) + small_ref[4:5, :]
        for t in range(4):
            total += jnp.dot(mixed_ref[t, rs, :], wo_rows(place ^ t), preferred_element_type=f32)
        centered = total - jnp.mean(total, -1, keepdims=True)
        rstd = lax.rsqrt(jnp.mean(centered * centered, -1, keepdims=True) + norm_epsilon)
        xhat = centered * rstd
        xhat_v[rs, :] = xhat
        rstd_v[rs, :] = jnp.broadcast_to(rstd, (tile, 128))
        hid_v[rs, :] = (xhat * small_ref[0:1, :] + small_ref[1:2, :]).astype(bf16)
        return 0

    lax.fori_loop(0, tiles, norm_one, 0)
    pltpu.make_async_copy(wu_v, wu_v, wsem.at[1]).wait()
    pltpu.make_async_copy(wd_v, wd_v, wsem.at[2]).wait()

    def ffn(n, _):
        p, r = n // tiles, n % tiles
        rs = rowsl(r)
        up = jnp.dot(hid_v[rs, :], wu_v[p], preferred_element_type=f32) + small_ref[pl.ds(8 + p, 1), :]
        act, slope = gelu_parts(up)
        act = act.astype(bf16)
        act_v[p, rs, :] = act
        slope_v[p, rs, :] = slope
        part = jnp.dot(act, wd_v[p], preferred_element_type=f32)

        @pl.when(p == 0)
        def _():
            ffn_v[rs, :] = part

        @pl.when(p > 0)
        def _():
            ffn_v[rs, :] += part

        return 0

    lax.fori_loop(0, 4 * tiles, ffn, 0)
    zero = jnp.zeros((1, width), f32)

    def norm_two(r, sums):
        rs = rowsl(r)
        dg, db, dd = sums
        hidden = xhat_v[rs, :] * small_ref[0:1, :] + small_ref[1:2, :]
        total = hidden + (ffn_v[rs, :] + small_ref[7:8, :])
        centered = total - jnp.mean(total, -1, keepdims=True)
        rstd = lax.rsqrt(jnp.mean(centered * centered, -1, keepdims=True) + norm_epsilon)
        xhat = centered * rstd
        out_ref[rs, :] = (xhat * small_ref[5:6, :] + small_ref[6:7, :]).astype(bf16)
        dy = dout_ref[rs, :].astype(f32)
        dg = dg + jnp.sum(dy * xhat, 0, keepdims=True)
        db = db + jnp.sum(dy, 0, keepdims=True)
        dx = dy * small_ref[5:6, :]
        dx = rstd * (dx - jnp.mean(dx, -1, keepdims=True) - xhat * jnp.mean(dx * xhat, -1, keepdims=True))
        dhid_v[rs, :] = dx
        short = dx.astype(bf16)
        gffn_v[rs, :] = short
        dd = dd + jnp.sum(short.astype(f32), 0, keepdims=True)
        return dg, db, dd

    dg2, db2, dd = lax.fori_loop(0, tiles, norm_two, (zero, zero, zero))
    sgrad_ref[...] = jnp.zeros_like(sgrad_ref)
    sgrad_ref[5:6, :] = dg2
    sgrad_ref[6:7, :] = db2
    sgrad_ref[7:8, :] = dd
    nt = (((1,), (1,)), ((), ()))
    tn = (((0,), (0,)), ((), ()))
    pieces = width // tile

    def wait_stage(ref, sem):
        pltpu.make_async_copy(ref, ref, sem).wait()

    def back(p, _):
        def back_rows(r, total):
            rs = rowsl(r)
            ga = lax.dot_general(gffn_v[rs, :], wd_v[p], nt, preferred_element_type=f32)
            gup = (ga * slope_v[p, rs, :]).astype(bf16)
            gup_v[rs, :] = gup
            dhid_v[rs, :] += lax.dot_general(gup, wu_v[p], nt, preferred_element_type=f32)
            return total + jnp.sum(gup.astype(f32), 0, keepdims=True)

        sgrad_ref[pl.ds(8 + p, 1), :] = lax.fori_loop(0, tiles, back_rows, zero)

        @pl.when(p > 0)
        def _():
            wait_stage(stage_d, gsem.at[0])
            wait_stage(stage_u, gsem.at[1])

        for m in range(pieces):
            cs = slice(m * tile, (m + 1) * tile)
            stage_d[cs, :] = lax.dot_general(act_v[p, :, cs], gffn_v[...], tn, preferred_element_type=f32).astype(bf16)
        for jj in range(2):
            for q in range(4):
                src = stage_d.at[pl.ds(jj * 4 * rows + q * rows, rows)]
                dst = grads_ref.at[q ^ place, (2 * p + jj) ^ item, pl.ds(rows, rows)]
                pltpu.make_async_copy(src, dst, gsem.at[0]).start()
        for m in range(pieces):
            cs = slice(m * tile, (m + 1) * tile)
            stage_u[cs, :] = lax.dot_general(hid_v[:, cs], gup_v[...], tn, preferred_element_type=f32).astype(bf16)
        for j in range(items):
            src = stage_u.at[pl.ds(j * rows, rows)]
            dst = grads_ref.at[p ^ place, j ^ item, pl.ds(0, rows)]
            pltpu.make_async_copy(src, dst, gsem.at[1]).start()
        return 0

    lax.fori_loop(0, 4, back, 0)

    def norm_back(r, sums):
        rs = rowsl(r)
        dg, db, da = sums
        dy = dhid_v[rs, :]
        xhat = xhat_v[rs, :]
        dg = dg + jnp.sum(dy * xhat, 0, keepdims=True)
        db = db + jnp.sum(dy, 0, keepdims=True)
        dx = dy * small_ref[0:1, :]
        dx = rstd_v[rs, 0:1] * (dx - jnp.mean(dx, -1, keepdims=True) - xhat * jnp.mean(dx * xhat, -1, keepdims=True))
        first_ref[rs, :] = dx
        short = dx.astype(bf16)
        hid_v[rs, :] = short
        da = da + jnp.sum(short.astype(f32), 0, keepdims=True)
        for t in range(4):
            gmix_ref[t, rs, :] = lax.dot_general(short, wo_rows(place ^ t), nt, preferred_element_type=f32).astype(bf16)
        return dg, db, da

    dg1, db1, da = lax.fori_loop(0, tiles, norm_back, (zero, zero, zero))
    sgrad_ref[0:1, :] = dg1
    sgrad_ref[1:2, :] = db1
    sgrad_ref[4:5, :] = da
    for j in range(items):
        stage_o[j, pl.ds(rows, third)] = jnp.zeros((third, width), bf16)
    for t in range(4):
        q = place ^ t
        part = lax.dot_general(mixed_ref[t], hid_v[...], tn, preferred_element_type=f32).astype(bf16)
        stage_o[2 * q, pl.ds(0, rows)] = part[:rows]
        stage_o[2 * q + 1, pl.ds(0, rows)] = part[rows:]
    for j in range(items):
        for u in range(4):
            src = stage_o.at[j, pl.ds(u * third, third)]
            dst = grads_ref.at[u ^ place, j ^ item, pl.ds(2 * rows, third)]
            pltpu.make_async_copy(src, dst, gsem.at[2]).start()
    wait_stage(stage_d, gsem.at[0])
    wait_stage(stage_u, gsem.at[1])
    wait_stage(stage_o, gsem.at[2])


def middle(where_am_i, own, far, near, x, mixed, dout, small, tile=256):
    items, quarter, width = own.shape
    rows = quarter * 3 // 7
    tokens = x.shape[0]
    any_space = pl.BlockSpec(memory_space=pl.ANY)
    vmem = pl.BlockSpec(memory_space=pltpu.VMEM)
    square = (tokens, width)
    return pl.pallas_call(
        functools.partial(middle_kernel, (items, rows, width, tile), where_am_i),
        out_shape=(
            jax.ShapeDtypeStruct(square, bf16),
            jax.ShapeDtypeStruct(square, f32),
            jax.ShapeDtypeStruct((4, tokens, width // 4), bf16),
            jax.ShapeDtypeStruct((4, items, quarter, width), bf16),
            jax.ShapeDtypeStruct(small.shape, f32),
        ),
        in_specs=[any_space] * 3 + [vmem] * 4,
        out_specs=(vmem, vmem, vmem, any_space, vmem),
        scratch_shapes=[
            pltpu.VMEM((items, 4 * rows // 3, width), bf16),
            pltpu.VMEM((4, width, width), bf16),
            pltpu.VMEM((4, width, width), bf16),
            pltpu.VMEM(square, f32),
            pltpu.VMEM(square, bf16),
            pltpu.VMEM((4, tokens, width), bf16),
            pltpu.VMEM((4, tokens, width), f32),
            pltpu.VMEM(square, f32),
            pltpu.VMEM(square, bf16),
            pltpu.VMEM(square, bf16),
            pltpu.VMEM(square, f32),
            pltpu.VMEM((tokens, 128), f32),
            pltpu.VMEM((width, width), bf16),
            pltpu.VMEM((width, width), bf16),
            pltpu.VMEM((items, 4 * rows // 3, width), bf16),
            pltpu.SemaphoreType.DMA((3,)),
            pltpu.SemaphoreType.DMA((3,)),
        ],
        compiler_params=pltpu.CompilerParams(vmem_limit_bytes=60 << 20),
        cost_estimate=pl.CostEstimate(flops=60 * 10**9, bytes_accessed=10**7, transcendentals=0),
        name="middle",
    )(own, far, near, x, mixed, dout, small)


def swap(values, axis, bit):
    size = lax.axis_size(axis)
    return lax.ppermute(values, axis, [(i, i ^ bit) for i in range(size)])


def take(values, at, dim):
    return lax.dynamic_index_in_dim(values, at, dim, keepdims=False)


def add_short(a, b):
    return (a.astype(f32) + b.astype(f32)).astype(bf16)


def in_order(pieces, place):
    pieces = pieces.reshape(2, 2, *pieces.shape[1:])
    pieces = jnp.where(place % 2 == 1, pieces[:, ::-1], pieces)
    pieces = jnp.where(place // 2 == 1, pieces[::-1], pieces)
    return pieces.reshape(4, *pieces.shape[2:])


def from_group(shard):
    pair = jnp.stack([shard, swap(shard, "seq", 2)])
    near = swap(pair, "seq", 1)
    return jnp.stack([pair[0], near[0], pair[1], near[1]])


def layer_norm(values, gain, bias):
    average = jnp.mean(values, -1, keepdims=True)
    centered = values - average
    spread = jnp.mean(centered * centered, -1, keepdims=True)
    return centered * lax.rsqrt(spread + norm_epsilon) * gain + bias


def exact_gelu(values):
    return jax.nn.gelu(values, approximate=False)


def packed_columns(own):
    heads = own.shape[2]
    cols = []
    for h in range(heads):
        pair = [own[:, 2, h], own[:, 1, h]]
        cols += pair if h % 2 == 0 else pair[::-1]
    for p in range((heads + 1) // 2):
        odd = own[:, 0, 2 * p + 1] if 2 * p + 1 < heads else jnp.zeros_like(own[:, 0, 0])
        cols += [odd * HD**-0.5, own[:, 0, 2 * p] * HD**-0.5]
    return jnp.concatenate(cols, -1)


def natural_columns(values, heads):
    parts = [[], [], []]
    for h in range(heads):
        first, second = values[:, h * 128 : h * 128 + HD], values[:, h * 128 + HD : h * 128 + 128]
        base = (heads + h // 2) * 128
        if h % 2 == 0:
            parts[2].append(first)
            parts[1].append(second)
            parts[0].append(values[:, base + HD : base + 128] * HD**-0.5)
        else:
            parts[1].append(first)
            parts[2].append(second)
            parts[0].append(values[:, base : base + HD] * HD**-0.5)
    return jnp.concatenate(parts[0] + parts[1] + parts[2], -1)


def adam_update(weight, first, second, grad, decay, rate):
    first_new = beta_first * first + (1.0 - beta_first) * grad
    second_new = beta_second * second + (1.0 - beta_second) * grad * grad
    first_hat = first_new / (1.0 - beta_first**ADAM_STEP)
    second_hat = second_new / (1.0 - beta_second**ADAM_STEP)
    weight_new = weight - rate * (
        first_hat / (jnp.sqrt(second_hat) + adam_epsilon) + decay * weight
    )
    return (weight_new, first_new, second_new)


def on_device(
    inputs,
    d_output,
    glob_count,
    glob_pos,
    rand_blocks,
    w_qkv,
    w_out,
    w_up,
    w_down,
    small_params,
    first_qkv,
    second_qkv,
    first_out,
    second_out,
    first_up,
    second_up,
    first_down,
    second_down,
    first_small,
    second_small,
):
    items_n, tok_rows, width = inputs.shape
    groups = lax.axis_size("seq")
    items = lax.axis_size("item")
    place = lax.axis_index("seq")
    heads = rand_blocks.shape[1]
    rows = w_out.shape[0]
    third = rows // 3

    def where_am_i():
        return lax.axis_index("item"), lax.axis_index("seq")

    def item_of():
        return lax.axis_index("item")

    own = take(w_qkv.reshape(-1, 3, groups, heads, HD), place, 2)
    piece = packed_columns(own).astype(bf16)
    pieces = [piece] + [swap(piece, "item", k) for k in range(1, items)]
    tokens_b = inputs.reshape(tok_rows, width)
    tokens_far = swap(tokens_b, "seq", 2)
    tokens_near = swap(tokens_b, "seq", 1)
    tokens_cross = swap(tokens_far, "seq", 1)
    xs = [tokens_b, tokens_near, tokens_far, tokens_cross]
    quarter = jnp.concatenate(
        [
            take(w_up.reshape(rows, 4, width), place, 1),
            take(w_down.reshape(4, rows, width), place, 0),
            take(w_out.reshape(3, third, width), jnp.minimum(place, 2), 0),
        ],
        0,
    ).astype(bf16)
    w_parts = [quarter] + [swap(quarter, "item", k) for k in range(1, items)]
    bias3 = jnp.stack([small_params[2], jnp.zeros((width,), f32), small_params[3]])
    slab_bias = packed_columns(take(bias3.reshape(1, 3, groups, heads, HD), place, 2))
    qkv, slab = project(item_of, xs, pieces, slab_bias)
    w_parts, qkv = lax.optimization_barrier((w_parts, qkv))
    idx, bias, gl = slots(glob_count[0], glob_pos[0], rand_blocks[0], place)
    mix2, mix3, lse_far = attn_fwd(idx, gl, qkv, bias, heads, 2, 2)
    w_parts, mix2, mix3, qkv = lax.optimization_barrier((w_parts, mix2, mix3, qkv))
    w_own = jnp.stack(w_parts)
    w_far = swap(w_own, "seq", 2)
    mix0, mix1, lse_near = attn_fwd(idx, gl, qkv, bias, heads, 0, 2)
    w_own, w_far, mix0, mix1, mix2, mix3 = lax.optimization_barrier(
        (w_own, w_far, mix0, mix1, mix2, mix3)
    )
    w_near = swap(jnp.stack([w_own, w_far]), "seq", 1)
    mixed = jnp.stack([mix0, swap(mix1, "seq", 1), swap(mix2, "seq", 2), swap(mix3, "seq", 3)])
    outputs, grad_first, grad_mixed, parts, small_part = middle(
        where_am_i, w_own, w_far, w_near, tokens_b, mixed, d_output.reshape(tok_rows, width), small_params
    )
    grads_in = [grad_mixed[0]] + [swap(grad_mixed[t], "seq", t) for t in range(1, 4)]
    parts = parts.reshape(2, 2, *parts.shape[1:])
    pair_sum = add_short(parts[:, 0], swap(parts[:, 1], "seq", 1))
    far_half = swap(pair_sum[1], "seq", 2)
    acc, dq_near = attn_bwd(idx, gl, qkv, bias, grads_in[:2], lse_near, heads, 0, (), False)
    far_half, acc, dq_near = lax.optimization_barrier((far_half, acc, dq_near))
    far_sum = add_short(pair_sum[0], far_half)
    received = [swap(far_sum[k], "item", k) for k in range(1, items)]
    grad_qkv = attn_bwd(idx, gl, qkv, bias, grads_in[2:], lse_far, heads, 2, (acc, dq_near), True)
    received, far_sum, grad_qkv = lax.optimization_barrier((received, far_sum, grad_qkv))
    shard = far_sum[0].astype(f32)
    for k in range(1, items):
        shard = shard + received[k - 1].astype(f32)
    small16 = jnp.pad(small_part, ((0, 4), (0, 0)))
    grad_inputs, slab_group, small_total, squares = tail(xs, grad_qkv, slab, grad_first, small16, shard, items, heads * 128)
    slab_group = in_order(slab_group, place)
    lines = natural_columns(slab_group[:, rows] + slab_group[:, rows + 1], heads).reshape(groups, 3, heads * HD)
    lines = lines.transpose(1, 0, 2).reshape(3, width)
    small_total = small_total[:12].at[2].set(lines[0]).at[3].set(lines[2])
    matrix_squares = squares[0, 0]
    group = in_order(from_group(shard), place)
    shard_up = group[:, :rows].transpose(1, 0, 2).reshape(rows, 4 * width)
    shard_down = group[:, rows : 2 * rows].reshape(4 * rows, width)
    shard_out = group[:3, 2 * rows :].reshape(rows, width)
    shard_qkv = (
        natural_columns(slab_group[:, :rows].reshape(groups * rows, -1), heads)
        .reshape(groups, rows, 3, heads * HD)
        .transpose(1, 2, 0, 3)
        .reshape(rows, 3 * width)
    )
    grad_norm = jnp.sqrt(matrix_squares + jnp.sum(small_total * small_total))
    factor = jnp.minimum(1.0, clip_level / (grad_norm + 1e-06))
    new_qkv = adam_update(
        w_qkv, first_qkv, second_qkv, shard_qkv * factor, weight_decay, learn_rate
    )
    new_out = adam_update(
        w_out, first_out, second_out, shard_out * factor, weight_decay, learn_rate
    )
    new_up = adam_update(w_up, first_up, second_up, shard_up * factor, weight_decay, learn_rate)
    new_down = adam_update(
        w_down, first_down, second_down, shard_down * factor, weight_decay, learn_rate
    )
    new_small = adam_update(
        small_params, first_small, second_small, small_total * factor, 0.0, small_rate
    )
    return (
        outputs.astype(bf16).reshape(items_n, tok_rows, width),
        grad_inputs.reshape(items_n, tok_rows, width),
        grad_norm,
        new_qkv[0],
        new_qkv[1],
        new_qkv[2],
        new_out[0],
        new_out[1],
        new_out[2],
        new_up[0],
        new_up[1],
        new_up[2],
        new_down[0],
        new_down[1],
        new_down[2],
        new_small[0],
        new_small[1],
        new_small[2],
    )


def on_device_many(
    inputs,
    d_output,
    glob_count,
    glob_pos,
    rand_blocks,
    w_qkv,
    w_out,
    w_up,
    w_down,
    small_params,
    first_qkv,
    second_qkv,
    first_out,
    second_out,
    first_up,
    second_up,
    first_down,
    second_down,
    first_small,
    second_small,
):
    items_n, tok_rows, width = inputs.shape
    groups = lax.axis_size("seq")
    place = lax.axis_index("seq")
    heads = rand_blocks.shape[1]
    row_count = tok_rows

    own = lax.dynamic_index_in_dim(
        w_qkv.reshape(-1, 3, groups, heads, HD), place, 2, keepdims=False
    )
    slab = lax.all_gather(packed_columns(own).astype(bf16), "item", axis=0, tiled=True)
    full_out, full_up, full_down = (
        lax.all_gather(w_out.astype(bf16), "item", axis=0, tiled=True),
        lax.all_gather(w_up.astype(bf16), "item", axis=0, tiled=True),
        lax.all_gather(w_down.astype(bf16), "item", axis=0, tiled=True),
    )
    bias3 = jnp.stack([small_params[2], jnp.zeros((width,), f32), small_params[3]])
    own_bias = lax.dynamic_index_in_dim(
        bias3.reshape(1, 3, groups, heads, HD), place, 2, keepdims=False
    )
    slab_bias = packed_columns(own_bias)
    tokens_b = inputs.reshape(tok_rows, width)
    tokens_all = lax.all_gather(tokens_b, "seq", axis=0, tiled=True)
    tokens_f = tokens_b.astype(f32)
    qkv = (jnp.dot(tokens_all, slab, preferred_element_type=f32) + slab_bias).astype(bf16)
    idx, bias, gl = slots(glob_count[0], glob_pos[0], rand_blocks[0], jnp.int32(0))
    *mixed_parts, lse = attn_fwd(idx, gl, qkv, bias, heads, 0, 4)
    mixed_heads = jnp.concatenate(mixed_parts, 0)
    mixed = lax.all_to_all(mixed_heads, "seq", split_axis=0, concat_axis=1, tiled=True)
    attn_out = jnp.dot(mixed, full_out, preferred_element_type=f32) + small_params[4]
    hidden, norm_one_back = jax.vjp(
        layer_norm, tokens_f + attn_out, small_params[0], small_params[1]
    )
    hidden_b = hidden.astype(bf16)
    up_pre = jnp.dot(hidden_b, full_up, preferred_element_type=f32) + small_params[8:12].reshape(-1)
    active, gelu_back = jax.vjp(exact_gelu, up_pre)
    active_b = active.astype(bf16)
    ffn_out = jnp.dot(active_b, full_down, preferred_element_type=f32) + small_params[7]
    outputs, norm_two_back = jax.vjp(layer_norm, hidden + ffn_out, small_params[5], small_params[6])
    grad_second, grad_gain_two, grad_bias_two = norm_two_back(
        d_output.reshape(row_count, width).astype(f32)
    )
    grad_ffn = grad_second.astype(bf16)
    grad_w_down = jnp.einsum("rf,rd->fd", active_b, grad_ffn, preferred_element_type=f32)
    grad_active = jnp.einsum("rd,fd->rf", grad_ffn, full_down, preferred_element_type=f32)
    (grad_up_pre,) = gelu_back(grad_active)
    grad_up_b = grad_up_pre.astype(bf16)
    grad_w_up = jnp.einsum("rd,rf->df", hidden_b, grad_up_b, preferred_element_type=f32)
    grad_hidden = grad_second + jnp.einsum(
        "rf,df->rd", grad_up_b, full_up, preferred_element_type=f32
    )
    grad_first, grad_gain_one, grad_bias_one = norm_one_back(grad_hidden)
    grad_attn = grad_first.astype(bf16)
    grad_w_out = jnp.einsum("rm,rd->md", mixed, grad_attn, preferred_element_type=f32)
    grad_mixed = jnp.einsum("rd,md->rm", grad_attn, full_out, preferred_element_type=f32).astype(
        bf16
    )
    grad_heads = lax.all_to_all(grad_mixed, "seq", split_axis=1, concat_axis=0, tiled=True)
    grads_in = [grad_heads[t * tok_rows : (t + 1) * tok_rows] for t in range(4)]
    grad_qkv = attn_bwd(idx, gl, qkv, bias, grads_in, lse, heads, 0, (), True)
    grad_slab = jnp.einsum("rd,re->de", tokens_all, grad_qkv, preferred_element_type=f32)
    grad_tokens = jnp.einsum("re,de->rd", grad_qkv, slab, preferred_element_type=f32).astype(bf16)
    grad_inputs = grad_first + lax.psum_scatter(
        grad_tokens, "seq", scatter_dimension=0, tiled=True
    ).astype(f32)
    slab_sum = natural_columns(jnp.sum(grad_qkv.astype(f32), 0)[None], heads)[0]
    bias_grads = lax.dynamic_update_index_in_dim(
        jnp.zeros((3, groups, heads * HD), f32), slab_sum.reshape(3, heads * HD), place, 1
    ).reshape(3, width)
    small_rows = jnp.stack(
        [
            grad_gain_one,
            grad_bias_one,
            bias_grads[0],
            bias_grads[2],
            jnp.sum(grad_attn.astype(f32), 0),
            grad_gain_two,
            grad_bias_two,
            jnp.sum(grad_ffn.astype(f32), 0),
        ]
    )
    small_part = jnp.concatenate(
        [small_rows, jnp.sum(grad_up_b.astype(f32), 0).reshape(4, width)], 0
    )
    small_total = lax.psum(small_part, ("item", "seq"))
    shard_down = lax.psum_scatter(grad_w_down.astype(bf16), "item", scatter_dimension=0, tiled=True)
    shard_up = lax.psum_scatter(grad_w_up.astype(bf16), "item", scatter_dimension=0, tiled=True)
    shard_out = lax.psum_scatter(grad_w_out.astype(bf16), "item", scatter_dimension=0, tiled=True)
    shard_slab = lax.psum_scatter(grad_slab.astype(bf16), "item", scatter_dimension=0, tiled=True)
    shard_slab = natural_columns(shard_slab.astype(f32), heads).reshape(-1, 3, 1, heads * HD)
    shard_qkv = lax.all_gather(shard_slab, "seq", axis=2, tiled=True).reshape(-1, 3 * width)
    shard_out, shard_up, shard_down = lax.psum(
        (shard_out.astype(f32), shard_up.astype(f32), shard_down.astype(f32)), "seq"
    )
    local_squares = (
        jnp.sum(shard_qkv * shard_qkv)
        + jnp.sum(shard_out * shard_out)
        + jnp.sum(shard_up * shard_up)
        + jnp.sum(shard_down * shard_down)
    )
    matrix_squares = lax.psum(local_squares, "item")
    grad_norm = jnp.sqrt(matrix_squares + jnp.sum(small_total * small_total))
    factor = jnp.minimum(1.0, clip_level / (grad_norm + 1e-06))
    new_qkv = adam_update(
        w_qkv, first_qkv, second_qkv, shard_qkv * factor, weight_decay, learn_rate
    )
    new_out = adam_update(
        w_out, first_out, second_out, shard_out * factor, weight_decay, learn_rate
    )
    new_up = adam_update(w_up, first_up, second_up, shard_up * factor, weight_decay, learn_rate)
    new_down = adam_update(
        w_down, first_down, second_down, shard_down * factor, weight_decay, learn_rate
    )
    new_small = adam_update(
        small_params, first_small, second_small, small_total * factor, 0.0, small_rate
    )
    return (
        outputs.astype(bf16).reshape(items_n, tok_rows, width),
        grad_inputs.reshape(items_n, tok_rows, width),
        grad_norm,
        new_qkv[0],
        new_qkv[1],
        new_qkv[2],
        new_out[0],
        new_out[1],
        new_out[2],
        new_up[0],
        new_up[1],
        new_up[2],
        new_down[0],
        new_down[1],
        new_down[2],
        new_small[0],
        new_small[1],
        new_small[2],
    )


def solution(mesh):
    few = mesh.shape["item"] == 8 and mesh.shape["seq"] == 4
    return jax.shard_map(
        on_device if few else on_device_many,
        mesh=mesh,
        in_specs=(
            P("item", "seq", None),
            P("item", "seq", None),
            P("item"),
            P("item", None),
            P("item", "seq", None, None),
            P("item", None),
            P("item", None),
            P("item", None),
            P("item", None),
            P(),
            P("item", None),
            P("item", None),
            P("item", None),
            P("item", None),
            P("item", None),
            P("item", None),
            P("item", None),
            P("item", None),
            P(),
            P(),
        ),
        out_specs=(
            P("item", "seq", None),
            P("item", "seq", None),
            P(),
            P("item", None),
            P("item", None),
            P("item", None),
            P("item", None),
            P("item", None),
            P("item", None),
            P("item", None),
            P("item", None),
            P("item", None),
            P("item", None),
            P("item", None),
            P("item", None),
            P(),
            P(),
            P(),
        ),
        check_vma=False,
    )
```

time: 818 us -> 586 us (0.72)
  blocking collectives: 202 us -> 0 us
  Pallas kernels: 153 us -> 288 us
  matrix products: 110 us -> 0 us
  waiting for transfers between devices: 248 us -> 154 us
  starting transfers between devices: 5.23 us -> 57.8 us
  between operations: 20.8 us -> 4.94 us
  local copies, waits for them, and re-layouts: 29.4 us -> 42.3 us
  other arithmetic: 41.1 us -> 31 us
    reduce_scatter x4 -> x0, waiting for transfers between devices: 169 us -> none  [the longest x1 99.1 us: on_device(): lax.psum_scatter(grad_w_up.astype(bf16), 'item', scatter_dimension=0, til...]
    ppermute x0 -> x36, waiting for transfers between devices: none -> 154 us  [swap(): return lax.ppermute(values, axis, [(i, i ^ bit) for i in range(size)])]
    psum x3 -> x0, blocking collectives: 137 us -> none  [the longest x1 75.1 us: on_device(): lax.psum((shard_out.astype(f32), shard_up.astype(f32), shard_down.astype(...]
    pallas_call x2 -> x7, Pallas kernels: 153 us -> 288 us  [the longest x2 84.5 us: attn_bwd(): pl.pallas_call(functools.partial(bwd_kernel, dims), out_shape=out_shape,...]
    dot_general x12 -> x0, matrix products: 110 us -> none  [the longest x1 28.8 us: on_device(): jnp.dot(hidden_b, full_up, preferred_element_type=f32)]
    all_gather x4 -> x0, waiting for transfers between devices: 64.7 us -> none  [the longest x1 51.8 us: on_device(): lax.all_gather(w_down.astype(bf16), 'item', axis=0, tiled=True)]
    ppermute x0 -> x36, starting transfers between devices: none -> 57.8 us  [swap(): return lax.ppermute(values, axis, [(i, i ^ bit) for i in range(size)])]
    all_gather x2 -> x0, blocking collectives: 46.2 us -> none  [the longest x1 34.5 us: on_device(): lax.all_gather(packed_columns(own).astype(bf16), 'item', axis=0, tiled=True)]
  transfers between devices with their start and end apart: 10 -> 36, of which waited for: 5 -> 15; matrix products, arithmetic and copies ran while one was open for 16% -> 5% of each run, Pallas kernels for 19% -> 23%
where the time goes in v2:
time: 586 us; the launch traced here: 577 us
  Pallas kernels  288 us (49%)
  waiting for transfers between devices  154 us (26%)
  starting transfers between devices  57.8 us (10%)
  local copies, waits for them, and re-layouts  42.3 us (7%)
  other arithmetic  31 us (5%)
    ppermute x36, waiting for transfers between devices, swap(): return lax.ppermute(values, axis, [(i, i ^ bit) for i in range(size)])  154 us
    pallas_call x2, Pallas kernels, attn_bwd(): pl.pallas_call(functools.partial(bwd_kernel, dims), out_shape=out_shape,...  84.5 us
    pallas_call x2, Pallas kernels, attn_fwd(): pl.pallas_call(functools.partial(fwd_kernel, dims), out_shape=tuple([jax....  79.6 us
    pallas_call x1, Pallas kernels, tail(): pl.pallas_call(functools.partial(tail_kernel, items, query_columns), out_...  65.4 us
    ppermute x36, starting transfers between devices, swap(): return lax.ppermute(values, axis, [(i, i ^ bit) for i in range(size)])  57.8 us
    pallas_call x1, Pallas kernels, middle(): pl.pallas_call(functools.partial(middle_kernel, (items, rows, width, tile...  48.6 us
    unnamed x103, local copies, waits for them, and re-layouts  18.7 us
  transfers between devices with their start and end apart: 36, of which 15 were waited for; matrix products, arithmetic and copies ran while one was open for 5% of the time, Pallas kernels for 23%

profile of v2, /device:TPU:0, one launch (start us, length us, event | category | flops | bytes accessed | tf_op | source)
XLA Modules:
  0.0 577.1 jit_solution(2268851215541803882)
XLA Ops:
  12.0 18.6 %collective-permute-done.8.refs_2_.x2 = bf16[768,768]{1,0:T(8,128)(2,1)} collective-permute-done((bf16[768,768]{1,0:T(8,128)(2,1)}, bf16[768,768]{1,0:T(8,128)(2,1)}, u32[]{:S(2)}, u32[]{:S(2)}) %collective-permute-start.8) | collective-permute-done | bytes 1179680 | tf_op jit(solution)/shard_map/ppermute | solution.py:914
  38.7 3.7 collective-permute-start.15
  43.3 5.5 collective-permute-done.13.refs_8_
  60.1 6.6 %collective-permute-done.16.refs_11_ = bf16[96,640]{1,0:T(8,128)(2,1)S(1)} collective-permute-done((bf16[96,640]{1,0:T(8,128)(2,1)S(1)}, bf16[96,640]{1,0:T(8,128)(2,1)S(1)}, u32[]{:S(2)}, u32[]{:S(2)}) %collective-permute-start.16) | collective-permute-done | bytes 122912 | tf_op jit(solution)/shard_map/ppermute | solution.py:914
  74.3 9.4 %project.1 = (bf16[3072,640]{1,0:T(8,128)(2,1)}, bf16[768,640]{1,0:T(8,128)(2,1)S(1)}) custom-call(bf16[768,768]{1,0:T(8,128)(2,1)S(1)} %bitcast.169, bf16[768,768]{1,0:T(8,128)(2,1)S(1)} %collective-permute-done.7.refs_1_.x1, bf16[768,768]{1,0:T(8,128)(2,1)} %collective-permute-done.8.refs_2_.x2, bf16[768,768]{1,0:T(8,128)(2,1)} %collective-permute-done.9.refs_3_.x3, ...), custom_call_target="tpu_custom_call" | custom-call | flops 6000000000 | bytes 10000000 | tf_op jit(solution)/shard_map/project/pallas_call | solution.py:586
  84.7 23.6 %collective-permute-done.3 = bf16[224,768]{1,0:T(8,128)(2,1)S(1)} collective-permute-done((bf16[224,768]{1,0:T(8,128)(2,1)}, bf16[224,768]{1,0:T(8,128)(2,1)S(1)}, u32[]{:S(2)}, u32[]{:S(2)}) %collective-permute-start.3) | collective-permute-done | bytes 344096 | tf_op jit(solution)/shard_map/ppermute | solution.py:914
  108.3 8.2 %collective-permute-done.4 = bf16[224,768]{1,0:T(8,128)(2,1)S(1)} collective-permute-done((bf16[224,768]{1,0:T(8,128)(2,1)}, bf16[224,768]{1,0:T(8,128)(2,1)S(1)}, u32[]{:S(2)}, u32[]{:S(2)}) %collective-permute-start.4) | collective-permute-done | bytes 344096 | tf_op jit(solution)/shard_map/ppermute | solution.py:914
  116.4 40.3 %attn_fwd.2 = (bf16[768,192]{1,0:T(8,128)(2,1)}, bf16[768,192]{1,0:T(8,128)(2,1)}, f32[1536,128]{1,0:T(8,128)}) custom-call(s32[1440]{0:T(1024)} %fusion.27.idx_ref, s32[5]{0:T(128)} %pad_add_fusion.2.gl_ref, bf16[3072,640]{1,0:T(8,128)(2,1)} %get-tuple-element.119.qkv_ref, f32[144,640]{1,0:T(8,128)} %reshape.371.bias_ref), custom_call_target="tpu_custom_call" | custom-call | flops 20000000000 | bytes 10000000 | tf_op jit(solution)/shard_map/attn_fwd/pallas_call | solution.py:178
  160.0 39.3 %attn_fwd.3 = (bf16[768,192]{1,0:T(8,128)(2,1)}, bf16[768,192]{1,0:T(8,128)(2,1)}, f32[1536,128]{1,0:T(8,128)}) custom-call(s32[1440]{0:T(1024)} %fusion.27.idx_ref, s32[5]{0:T(128)} %pad_add_fusion.2.gl_ref, bf16[3072,640]{1,0:T(8,128)(2,1)} %get-tuple-element.119.qkv_ref, f32[144,640]{1,0:T(8,128)} %reshape.371.bias_ref), custom_call_target="tpu_custom_call" | custom-call | flops 20000000000 | bytes 10000000 | tf_op jit(solution)/shard_map/attn_fwd/pallas_call | solution.py:178
  199.3 19.6 %collective-permute-done.17.far_ref = bf16[8,224,768]{2,1,0:T(8,128)(2,1)S(1)} collective-permute-done((bf16[8,224,768]{2,1,0:T(8,128)(2,1)S(1)}, bf16[8,224,768]{2,1,0:T(8,128)(2,1)S(1)}, u32[]{:S(2)}, u32[]{:S(2)}) %collective-permute-start.17) | collective-permute-done | bytes 2752544 | tf_op jit(solution)/shard_map/ppermute | solution.py:914
  222.6 8.6 %collective-permute-done.21 = bf16[768,192]{1,0:T(8,128)(2,1)S(1)} collective-permute-done((bf16[768,192]{1,0:T(8,128)(2,1)S(1)}, bf16[768,192]{1,0:T(8,128)(2,1)S(1)}, u32[]{:S(2)}, u32[]{:S(2)}) %collective-permute-start.21) | collective-permute-done | bytes 294944 | tf_op jit(solution)/shard_map/ppermute | solution.py:914
  231.3 9.1 %collective-permute-done.20 = bf16[768,192]{1,0:T(8,128)(2,1)S(1)} collective-permute-done((bf16[768,192]{1,0:T(8,128)(2,1)S(1)}, bf16[768,192]{1,0:T(8,128)(2,1)S(1)}, u32[]{:S(2)}, u32[]{:S(2)}) %collective-permute-start.20) | collective-permute-done | bytes 294944 | tf_op jit(solution)/shard_map/ppermute | solution.py:914
  244.3 48.6 %middle.1 = (bf16[768,768]{1,0:T(8,128)(2,1)}, f32[768,768]{1,0:T(8,128)}, bf16[4,768,192]{2,1,0:T(8,128)(2,1)}, bf16[4,8,224,768]{3,2,1,0:T(8,128)(2,1)}, f32[12,768]{1,0:T(8,128)}) custom-call(bf16[8,224,768]{2,1,0:T(8,128)(2,1)} %copy-done.8, bf16[8,224,768]{2,1,0:T(8,128)(2,1)} %copy-done.9, bf16[2,8,224,768]{3,2,1,0:T(8,128)(2,1)} %copy-done.34, ...), custom_call_target="tpu_custom_call" | custom-call | flops 60000002048 | bytes 10000000 | tf_op jit(solution)/shard_map/middle/pallas_call | solution.py:876
  295.9 9.0 %collective-permute-done.22 = bf16[2,8,224,768]{3,2,1,0:T(8,128)(2,1)S(1)} collective-permute-done((bf16[2,8,224,768]{3,2,1,0:T(8,128)(2,1)S(1)}, bf16[2,8,224,768]{3,2,1,0:T(8,128)(2,1)S(1)}, u32[]{:S(2)}, u32[]{:S(2)}) %collective-permute-start.22) | collective-permute-done | bytes 5505056 | tf_op jit(solution)/shard_map/ppermute | solution.py:914
  305.0 4.2 fusion
  316.1 40.3 %attn_bwd.2 = (f32[3072,384]{1,0:T(8,128)}, bf16[1536,256]{1,0:T(8,128)(2,1)}) custom-call(s32[1440]{0:T(1024)} %fusion.27.idx_ref, s32[5]{0:T(128)} %pad_add_fusion.2.gl_ref, bf16[3072,640]{1,0:T(8,128)(2,1)} %get-tuple-element.119.qkv_ref, f32[144,640]{1,0:T(8,128)} %reshape.371.bias_ref, bf16[768,192]{1,0:T(8,128)(2,1)} %get-tuple-element.185.rest_0_, ...), custom_call_target="tpu_custom_call" | custom-call | flops 22000001024 | bytes 10000000 | tf_op jit(solution)/shard_map/attn_bwd/pallas_call | solution.py:335
  356.4 17.9 %collective-permute-done.23 = bf16[8,224,768]{2,1,0:T(8,128)(2,1)S(1)} collective-permute-done((bf16[8,224,768]{2,1,0:T(8,128)(2,1)}, bf16[8,224,768]{2,1,0:T(8,128)(2,1)S(1)}, u32[]{:S(2)}, u32[]{:S(2)}) %collective-permute-start.23) | collective-permute-done | bytes 2752544 | tf_op jit(solution)/shard_map/ppermute | solution.py:914
  380.9 15.3 %collective-permute-start.26 = (bf16[224,768]{1,0:T(8,128)(2,1)S(1)}, bf16[224,768]{1,0:T(8,128)(2,1)}, u32[]{:S(2)}, u32[]{:S(2)}) collective-permute-start(bf16[224,768]{1,0:T(8,128)(2,1)S(1)} %get-tuple-element.180), channel_id=1, source_target_pairs={{0,8},{4,12},{8,0},{12,4},{16,24},{20,28},{24,16},{28,20},{1,9},{5... | collective-permute-start | bytes 1032200 | tf_op jit(solution)/shard_map/ppermute | solution.py:914
  399.3 8.9 %collective-permute-done.32.rest_0_ = bf16[768,192]{1,0:T(8,128)(2,1)S(1)} collective-permute-done((bf16[768,192]{1,0:T(8,128)(2,1)S(1)}, bf16[768,192]{1,0:T(8,128)(2,1)S(1)}, u32[]{:S(2)}, u32[]{:S(2)}) %collective-permute-start.32) | collective-permute-done | bytes 294944 | tf_op jit(solution)/shard_map/ppermute | solution.py:914
  413.2 3.8 collective-permute-start.29
  420.7 44.2 %attn_bwd.3.gq_ref = bf16[3072,640]{1,0:T(8,128)(2,1)} custom-call(s32[1440]{0:T(1024)} %fusion.27.idx_ref, s32[5]{0:T(128)} %pad_add_fusion.2.gl_ref, bf16[3072,640]{1,0:T(8,128)(2,1)} %get-tuple-element.119.qkv_ref, f32[144,640]{1,0:T(8,128)} %reshape.371.bias_ref, bf16[768,192]{1,0:T(8,128)(2,1)} %copy-done.37, bf16[768,192]{1,0:T(8,128)(2,1)} %copy-done.38, ...), custom_call_target="tpu_custom_call" | custom-call | flops 22000001024 | bytes 10000000 | tf_op jit(solution)/shard_map/attn_bwd/pallas_call | solution.py:335
  467.5 65.4 %tail.1 = (f32[768,768]{1,0:T(8,128)}, f32[4,112,640]{2,1,0:T(8,128)}, f32[16,768]{1,0:T(8,128)}, f32[8,128]{1,0:T(8,128)}) custom-call(bf16[768,768]{1,0:T(8,128)(2,1)} %bitcast.168, bf16[768,768]{1,0:T(8,128)(2,1)} %copy-done.1, bf16[768,768]{1,0:T(8,128)(2,1)} %collective-permute-done.8.refs_2_.x2, bf16[768,768]{1,0:T(8,128)(2,1)} %collective-permute-done.9.refs_3_.x3, ...), custom_call_target="tpu_custom_call" | custom-call | flops 60000002048 | bytes 10000000 | tf_op jit(solution)/shard_map/tail/pallas_call | solution.py:529
  542.0 10.9 %collective-permute-done.34 = f32[224,768]{1,0:T(8,128)S(1)} collective-permute-done((f32[224,768]{1,0:T(8,128)S(1)}, f32[224,768]{1,0:T(8,128)S(1)}, u32[]{:S(2)}, u32[]{:S(2)}) %collective-permute-start.34) | collective-permute-done | bytes 688160 | tf_op jit(solution)/shard_map/ppermute | solution.py:914
  559.7 3.6 multiply_subtract_fusion.2
  (260 shorter events, 107.6 us)
Async XLA Ops:
  0.7 69.9 %collective-permute-start.7 = (bf16[768,768]{1,0:T(8,128)(2,1)}, bf16[768,768]{1,0:T(8,128)(2,1)S(1)}, u32[]{:S(2)}, u32[]{:S(2)}) collective-permute-start(bf16[768,768]{1,0:T(8,128)(2,1)} %bitcast.165), channel_id=1, source_target_pairs={{0,1},{1,0},{2,3},{3,2},{4,5},{5,4},{6,7},{7,6},{8,9},{9,8},{10,11... | collective-permute-start | bytes 3538952 | tf_op jit(solution)/shard_map/ppermute | solution.py:914
  1.2 29.5 %collective-permute-start.8 = (bf16[768,768]{1,0:T(8,128)(2,1)}, bf16[768,768]{1,0:T(8,128)(2,1)}, u32[]{:S(2)}, u32[]{:S(2)}) collective-permute-start(bf16[768,768]{1,0:T(8,128)(2,1)} %bitcast.166), channel_id=1, source_target_pairs={{0,2},{1,3},{2,0},{3,1},{4,6},{5,7},{6,4},{7,5},{8,10},{9,11},{10,... | collective-permute-start | bytes 3538952 | tf_op jit(solution)/shard_map/ppermute | solution.py:914
  5.8 27.8 %collective-permute-start.10 = (bf16[96,640]{1,0:T(8,128)(2,1)S(1)}, bf16[96,640]{1,0:T(8,128)(2,1)S(1)}, u32[]{:S(2)}, u32[]{:S(2)}) collective-permute-start(bf16[96,640]{1,0:T(8,128)(2,1)S(1)} %concatenate.37.refs_4_), channel_id=1, source_target_pairs={{0,4},{4,0},{8,12},{12,8},{16,20},{20,16},{24,28},{28,24},{1,5},{5... | collective-permute-start | bytes 368648 | tf_op jit(solution)/shard_map/ppermute | solution.py:914
  7.4 29.2 %collective-permute-start.11 = (bf16[96,640]{1,0:T(8,128)(2,1)S(1)}, bf16[96,640]{1,0:T(8,128)(2,1)S(1)}, u32[]{:S(2)}, u32[]{:S(2)}) collective-permute-start(bf16[96,640]{1,0:T(8,128)(2,1)S(1)} %concatenate.37.refs_4_), channel_id=1, source_target_pairs={{0,8},{4,12},{8,0},{12,4},{16,24},{20,28},{24,16},{28,20},{1,9},{5... | collective-permute-start | bytes 368648 | tf_op jit(solution)/shard_map/ppermute | solution.py:914
  8.9 29.8 %collective-permute-start.12 = (bf16[96,640]{1,0:T(8,128)(2,1)S(1)}, bf16[96,640]{1,0:T(8,128)(2,1)S(1)}, u32[]{:S(2)}, u32[]{:S(2)}) collective-permute-start(bf16[96,640]{1,0:T(8,128)(2,1)S(1)} %concatenate.37.refs_4_), channel_id=1, source_target_pairs={{0,12},{4,8},{8,4},{12,0},{16,28},{20,24},{24,20},{28,16},{1,13},{... | collective-permute-start | bytes 368648 | tf_op jit(solution)/shard_map/ppermute | solution.py:914
  30.6 41.4 %collective-permute-start.9 = (bf16[768,768]{1,0:T(8,128)(2,1)}, bf16[768,768]{1,0:T(8,128)(2,1)}, u32[]{:S(2)}, u32[]{:S(2)}) collective-permute-start(bf16[768,768]{1,0:T(8,128)(2,1)} %collective-permute-done.8.refs_2_.x2), channel_id=1, source_target_pairs={{0,1},{1,0},{2,3},{3,2},{4,5},{5,4},{6,7},{7,6},{8,9},{9,8},{10,11... | collective-permute-start | bytes 3538952 | tf_op jit(solution)/shard_map/ppermute | solution.py:914
  48.7 17.9 %collective-permute-start = (bf16[224,768]{1,0:T(8,128)(2,1)}, bf16[224,768]{1,0:T(8,128)(2,1)}, u32[]{:S(2)}, u32[]{:S(2)}) collective-permute-start(bf16[224,768]{1,0:T(8,128)(2,1)} %pad_maximum_fusion.4), channel_id=1, source_target_pairs={{0,4},{4,0},{8,12},{12,8},{16,20},{20,16},{24,28},{28,24},{1,5},{5... | collective-permute-start | bytes 1032200 | tf_op jit(solution)/shard_map/ppermute | solution.py:914
  66.6 18.0 %collective-permute-start.2 = (bf16[224,768]{1,0:T(8,128)(2,1)}, bf16[224,768]{1,0:T(8,128)(2,1)S(1)}, u32[]{:S(2)}, u32[]{:S(2)}) collective-permute-start(bf16[224,768]{1,0:T(8,128)(2,1)} %pad_maximum_fusion.4), channel_id=1, source_target_pairs={{0,12},{4,8},{8,4},{12,0},{16,28},{20,24},{24,20},{28,16},{1,13},{... | collective-permute-start | bytes 1032200 | tf_op jit(solution)/shard_map/ppermute | solution.py:914
  66.7 41.6 %collective-permute-start.3 = (bf16[224,768]{1,0:T(8,128)(2,1)}, bf16[224,768]{1,0:T(8,128)(2,1)S(1)}, u32[]{:S(2)}, u32[]{:S(2)}) collective-permute-start(bf16[224,768]{1,0:T(8,128)(2,1)} %pad_maximum_fusion.4), channel_id=1, source_target_pairs={{0,16},{4,20},{8,24},{12,28},{16,0},{20,4},{24,8},{28,12},{1,17},{... | collective-permute-start | bytes 1032200 | tf_op jit(solution)/shard_map/ppermute | solution.py:914
  68.2 48.2 %collective-permute-start.4 = (bf16[224,768]{1,0:T(8,128)(2,1)}, bf16[224,768]{1,0:T(8,128)(2,1)S(1)}, u32[]{:S(2)}, u32[]{:S(2)}) collective-permute-start(bf16[224,768]{1,0:T(8,128)(2,1)} %pad_maximum_fusion.4), channel_id=1, source_target_pairs={{0,20},{4,16},{8,28},{12,24},{16,4},{20,0},{24,12},{28,8},{1,21},{... | collective-permute-start | bytes 1032200 | tf_op jit(solution)/shard_map/ppermute | solution.py:914
  70.5 45.9 %collective-permute-start.5 = (bf16[224,768]{1,0:T(8,128)(2,1)}, bf16[224,768]{1,0:T(8,128)(2,1)S(1)}, u32[]{:S(2)}, u32[]{:S(2)}) collective-permute-start(bf16[224,768]{1,0:T(8,128)(2,1)} %pad_maximum_fusion.4), channel_id=1, source_target_pairs={{0,24},{4,28},{8,16},{12,20},{16,8},{20,12},{24,0},{28,4},{1,25},{... | collective-permute-start | bytes 1032200 | tf_op jit(solution)/shard_map/ppermute | solution.py:914
  72.1 44.4 %collective-permute-start.6 = (bf16[224,768]{1,0:T(8,128)(2,1)}, bf16[224,768]{1,0:T(8,128)(2,1)S(1)}, u32[]{:S(2)}, u32[]{:S(2)}) collective-permute-start(bf16[224,768]{1,0:T(8,128)(2,1)} %pad_maximum_fusion.4), channel_id=1, source_target_pairs={{0,28},{4,24},{8,20},{12,16},{16,12},{20,8},{24,4},{28,0},{1,29},{... | collective-permute-start | bytes 1032200 | tf_op jit(solution)/shard_map/ppermute | solution.py:914
  159.9 59.0 %collective-permute-start.17 = (bf16[8,224,768]{2,1,0:T(8,128)(2,1)S(1)}, bf16[8,224,768]{2,1,0:T(8,128)(2,1)S(1)}, u32[]{:S(2)}, u32[]{:S(2)}) collective-permute-start(bf16[8,224,768]{2,1,0:T(8,128)(2,1)S(1)} %bitcast_dynamic-update-slice_fusion.own_ref), channel_id=1, source_target_pairs={{0,2},{1,3},{2,0},{3,1},{4,6},{5,7},{6,4},{7,5},{8,10},{9,11},{10,... | collective-permute-start | bytes 8257544 | tf_op jit(solution)/shard_map/ppermute | solution.py:914
  220.5 21.5 %collective-permute-start.18 = (bf16[2,8,224,768]{3,2,1,0:T(8,128)(2,1)S(1)}, bf16[2,8,224,768]{3,2,1,0:T(8,128)(2,1)S(1)}, u32[]{:S(2)}, u32[]{:S(2)}) collective-permute-start(bf16[2,8,224,768]{3,2,1,0:T(8,128)(2,1)S(1)} %pad_maximum_fusion), channel_id=1, source_target_pairs={{0,1},{1,0},{2,3},{3,2},{4,5},{5,4},{6,7},{7,6},{8,9},{9,8},{10,11... | collective-permute-start | bytes 16515080 | tf_op jit(solution)/shard_map/ppermute | solution.py:914
  220.9 19.4 %collective-permute-start.20 = (bf16[768,192]{1,0:T(8,128)(2,1)S(1)}, bf16[768,192]{1,0:T(8,128)(2,1)S(1)}, u32[]{:S(2)}, u32[]{:S(2)}) collective-permute-start(bf16[768,192]{1,0:T(8,128)(2,1)S(1)} %copy-done.35), channel_id=1, source_target_pairs={{0,2},{1,3},{2,0},{3,1},{4,6},{5,7},{6,4},{7,5},{8,10},{9,11},{10,... | collective-permute-start | bytes 884744 | tf_op jit(solution)/shard_map/ppermute | solution.py:914
  222.6 17.7 %collective-permute-start.19 = (bf16[768,192]{1,0:T(8,128)(2,1)S(1)}, bf16[768,192]{1,0:T(8,128)(2,1)S(1)}, u32[]{:S(2)}, u32[]{:S(2)}) collective-permute-start(bf16[768,192]{1,0:T(8,128)(2,1)S(1)} %copy-done.39), channel_id=1, source_target_pairs={{0,1},{1,0},{2,3},{3,2},{4,5},{5,4},{6,7},{7,6},{8,9},{9,8},{10,11... | collective-permute-start | bytes 884744 | tf_op jit(solution)/shard_map/ppermute | solution.py:914
  312.4 61.9 %collective-permute-start.23 = (bf16[8,224,768]{2,1,0:T(8,128)(2,1)}, bf16[8,224,768]{2,1,0:T(8,128)(2,1)S(1)}, u32[]{:S(2)}, u32[]{:S(2)}) collective-permute-start(bf16[8,224,768]{2,1,0:T(8,128)(2,1)} %slice_bitcast_fusion.2), channel_id=1, source_target_pairs={{0,2},{1,3},{2,0},{3,1},{4,6},{5,7},{6,4},{7,5},{8,10},{9,11},{10,... | collective-permute-start | bytes 8257544 | tf_op jit(solution)/shard_map/ppermute | solution.py:914
  380.4 36.7 %collective-permute-start.25 = (bf16[224,768]{1,0:T(8,128)(2,1)S(1)}, bf16[224,768]{1,0:T(8,128)(2,1)S(1)}, u32[]{:S(2)}, u32[]{:S(2)}) collective-permute-start(bf16[224,768]{1,0:T(8,128)(2,1)S(1)} %get-tuple-element.181), channel_id=1, source_target_pairs={{0,4},{4,0},{8,12},{12,8},{16,20},{20,16},{24,28},{28,24},{1,5},{5... | collective-permute-start | bytes 1032200 | tf_op jit(solution)/shard_map/ppermute | solution.py:914
  380.9 36.2 %collective-permute-start.26 = (bf16[224,768]{1,0:T(8,128)(2,1)S(1)}, bf16[224,768]{1,0:T(8,128)(2,1)}, u32[]{:S(2)}, u32[]{:S(2)}) collective-permute-start(bf16[224,768]{1,0:T(8,128)(2,1)S(1)} %get-tuple-element.180), channel_id=1, source_target_pairs={{0,8},{4,12},{8,0},{12,4},{16,24},{20,28},{24,16},{28,20},{1,9},{5... | collective-permute-start | bytes 1032200 | tf_op jit(solution)/shard_map/ppermute | solution.py:914
  397.9 67.1 %collective-permute-start.27 = (bf16[224,768]{1,0:T(8,128)(2,1)}, bf16[224,768]{1,0:T(8,128)(2,1)}, u32[]{:S(2)}, u32[]{:S(2)}) collective-permute-start(bf16[224,768]{1,0:T(8,128)(2,1)} %get-tuple-element.179), channel_id=1, source_target_pairs={{0,12},{4,8},{8,4},{12,0},{16,28},{20,24},{24,20},{28,16},{1,13},{... | collective-permute-start | bytes 1032200 | tf_op jit(solution)/shard_map/ppermute | solution.py:914
  408.3 56.7 %collective-permute-start.28 = (bf16[224,768]{1,0:T(8,128)(2,1)}, bf16[224,768]{1,0:T(8,128)(2,1)S(1)}, u32[]{:S(2)}, u32[]{:S(2)}) collective-permute-start(bf16[224,768]{1,0:T(8,128)(2,1)} %get-tuple-element.178), channel_id=1, source_target_pairs={{0,16},{4,20},{8,24},{12,28},{16,0},{20,4},{24,8},{28,12},{1,17},{... | collective-permute-start | bytes 1032200 | tf_op jit(solution)/shard_map/ppermute | solution.py:914
  413.2 51.7 %collective-permute-start.29 = (bf16[224,768]{1,0:T(8,128)(2,1)}, bf16[224,768]{1,0:T(8,128)(2,1)S(1)}, u32[]{:S(2)}, u32[]{:S(2)}) collective-permute-start(bf16[224,768]{1,0:T(8,128)(2,1)} %get-tuple-element.177), channel_id=1, source_target_pairs={{0,20},{4,16},{8,28},{12,24},{16,4},{20,0},{24,12},{28,8},{1,21},{... | collective-permute-start | bytes 1032200 | tf_op jit(solution)/shard_map/ppermute | solution.py:914
  417.1 47.9 %collective-permute-start.30 = (bf16[224,768]{1,0:T(8,128)(2,1)}, bf16[224,768]{1,0:T(8,128)(2,1)}, u32[]{:S(2)}, u32[]{:S(2)}) collective-permute-start(bf16[224,768]{1,0:T(8,128)(2,1)} %get-tuple-element.176), channel_id=1, source_target_pairs={{0,24},{4,28},{8,16},{12,20},{16,8},{20,12},{24,0},{28,4},{1,25},{... | collective-permute-start | bytes 1032200 | tf_op jit(solution)/shard_map/ppermute | solution.py:914
  417.1 47.8 %collective-permute-start.31 = (bf16[224,768]{1,0:T(8,128)(2,1)}, bf16[224,768]{1,0:T(8,128)(2,1)}, u32[]{:S(2)}, u32[]{:S(2)}) collective-permute-start(bf16[224,768]{1,0:T(8,128)(2,1)} %get-tuple-element.175), channel_id=1, source_target_pairs={{0,28},{4,24},{8,20},{12,16},{16,12},{20,8},{24,4},{28,0},{1,29},{... | collective-permute-start | bytes 1032200 | tf_op jit(solution)/shard_map/ppermute | solution.py:914
  (53 other events, 399.3 us)
